TPU v7x, 512 devices: a whole 4x8x8 slice. The times are simulated.
512 devices in a mesh: chain: 16 (over y, core), sector: 32 (over x, z).
Axes of the slice: x: 4, y: 8, z: 8, core: 2. Of those that a mesh axis runs over, the one named last changes fastest.
Arguments:
- left_sites: bfloat16 [16, 32, 256, 6, 256], P('chain', 'sector'), may hold values from -0.375 to 0.375
- right_sites: bfloat16 [16, 32, 256, 6, 256], P('chain', 'sector'), may hold values from -6 to 6
- pair_gates: bfloat16 [16, 36, 36], P('chain'), as said below
- test_matrix: bfloat16 [16, 32, 1536, 256], P('chain', 'sector'), may hold values from -0.15625 to 0.15625
- kept_columns: int32 [16, 32], P('chain', 'sector'), may hold values from 32 to 256, as said below
Outputs:
- new_left: bfloat16 [16, 32, 256, 6, 256], P('chain', 'sector')
- new_right: bfloat16 [16, 32, 256, 6, 256], P('chain', 'sector')
Inputs may be any that keep to these rules, and one draw needn't show every extreme that they name: pair_gates[c, p * 6 + q, n * 6 + r] is zero unless p + q = n + r. `kept_columns`: every bond has a sector that keeps all 256 columns.
All inputs are finite; a program needn't handle non-finite values.
Results may differ from a plain program's by a relative error of at most 0.0063.
Values may be sent and summed in bfloat16 or wider, within the bound.
A program may use at most 64 MiB of HBM per device.

v0:
```python
import math

import jax
import jax.numpy as jnp
from jax import lax
from jax.sharding import PartitionSpec as P

RIDGE_SHARE = 0.05
TINY_SHIFT = 1e-05


def shifted(array, axis, by):
    peers = lax.axis_size(axis)
    pairs = [(i, i + by) for i in range(peers) if 0 <= i + by < peers]
    return lax.ppermute(array, axis, pairs)


def orthonormal_basis(stacked, sketch_in, kept_count, rows_sector):
    first_sketch = jnp.dot(stacked, sketch_in, preferred_element_type=jnp.float32).astype(
        jnp.bfloat16
    )
    back_sketch = jnp.einsum(
        "rk,rc->kc", stacked, first_sketch, preferred_element_type=jnp.float32
    ).astype(jnp.bfloat16)
    sketch = jnp.dot(stacked, back_sketch, preferred_element_type=jnp.float32)
    gram_matrix = jnp.einsum("rc,rd->cd", sketch, sketch, precision=lax.Precision.HIGHEST)
    ridge_term = RIDGE_SHARE * jnp.trace(gram_matrix) / rows_sector + TINY_SHIFT
    gram_matrix = gram_matrix + ridge_term * jnp.eye(rows_sector, dtype=jnp.float32)
    factor = jnp.linalg.cholesky(gram_matrix)
    basis_cols = jax.scipy.linalg.solve_triangular(factor, sketch.T, lower=True).T
    column = jnp.arange(rows_sector, dtype=jnp.int32)
    return jnp.where(column[None, :] < kept_count, basis_cols, 0.0)


def per_device(left_sites, right_sites, pair_gates, test_matrix, kept_columns):
    rows_sector = left_sites.shape[2]
    photon_levels = left_sites.shape[3]
    sector_count = lax.axis_size("sector")
    sector_here = lax.axis_index("sector")
    chain_count = lax.axis_size("chain")
    chain_here = lax.axis_index("chain")
    basis_scale = math.sqrt(photon_levels * rows_sector)
    own_left = left_sites[0, 0]
    own_right = right_sites[0, 0]
    partner = shifted(own_right, "chain", -1)
    fetched = [partner]
    for offset in range(1, photon_levels):
        fetched.append(shifted(partner, "sector", -offset))
    photon_axis = jnp.arange(photon_levels, dtype=jnp.int32)
    partials = []
    for first_level in range(photon_levels):
        partial_value = jnp.dot(
            own_left[:, first_level, :],
            fetched[first_level].reshape(rows_sector, photon_levels * rows_sector),
            preferred_element_type=jnp.float32,
        )
        partial_value = partial_value.reshape(rows_sector, photon_levels, rows_sector)
        inside = sector_here + first_level + photon_axis < sector_count
        partials.append(jnp.where(inside[None, :, None], partial_value, 0.0).astype(jnp.bfloat16))
    product = jnp.stack(partials, axis=1).reshape(
        rows_sector, photon_levels * photon_levels, rows_sector
    )
    gate_rows = pair_gates[0].reshape(photon_levels, photon_levels, photon_levels * photon_levels)
    mixed_rows = []
    for photon in range(photon_levels):
        mixed_block = jnp.einsum(
            "qy,iyk->iqk", gate_rows[photon], product, preferred_element_type=jnp.float32
        )
        mixed_rows.append(mixed_block.astype(jnp.bfloat16))
    received = [mixed_rows[0]]
    for photon in range(1, photon_levels):
        received.append(shifted(mixed_rows[photon], "sector", photon))
    stacked = jnp.stack(received, axis=0).reshape(
        photon_levels * rows_sector, photon_levels * rows_sector
    )
    basis_cols = orthonormal_basis(stacked, test_matrix[0, 0], kept_columns[0, 0], rows_sector)
    scaled = (basis_cols * basis_scale).astype(jnp.bfloat16)
    fresh_right = jnp.einsum("rc,rk->ck", scaled, stacked, preferred_element_type=jnp.float32) * (
        1.0 / basis_scale
    )
    fresh_right = fresh_right.astype(jnp.bfloat16).reshape(rows_sector, photon_levels, rows_sector)
    pieces = scaled.reshape(photon_levels, rows_sector, rows_sector)
    returned = [pieces[0]]
    for photon in range(1, photon_levels):
        returned.append(shifted(pieces[photon], "sector", -photon))
    fresh_left = jnp.stack(returned, axis=1)
    new_left = jnp.where(chain_here == chain_count - 1, own_left, fresh_left)
    shipped = shifted(fresh_right, "chain", 1)
    new_right = jnp.where(chain_here == 0, own_right, shipped)
    return (new_left[None, None], new_right[None, None])


def solution(mesh):
    return jax.shard_map(
        per_device,
        mesh=mesh,
        in_specs=(
            P("chain", "sector", None, None, None),
            P("chain", "sector", None, None, None),
            P("chain", None, None),
            P("chain", "sector", None, None),
            P("chain", "sector"),
        ),
        out_specs=(P("chain", "sector", None, None, None), P("chain", "sector", None, None, None)),
        check_vma=False,
    )
```

profile of v0, /device:TPU:102, one launch (start us, length us, event | category | flops | bytes accessed | tf_op | source)
XLA Modules:
  0.0 512.9 jit_solution(14939370670314388801)
XLA Ops:
  4.8 8.8 %collective-permute-done = bf16[256,6,256]{0,2,1:T(8,128)(2,1)S(1)} collective-permute-done((bf16[256,6,256]{0,2,1:T(8,128)(2,1)S(1)}, bf16[256,6,256]{0,2,1:T(8,128)(2,1)S(1)}, u32[]{:S(2)}, u32[]{:S(2)}) %collective-permute-start) | collective-permute-done | bytes 786464 | tf_op jit(solution)/shard_map/ppermute | solution.py:15
  15.5 10.8 %collective-permute-start.2 = (bf16[256,6,256]{0,2,1:T(8,128)(2,1)S(1)}, bf16[256,6,256]{0,2,1:T(8,128)(2,1)}, u32[]{:S(2)}, u32[]{:S(2)}) collective-permute-start(bf16[256,6,256]{0,2,1:T(8,128)(2,1)S(1)} %collective-permute-done), channel_id=1, source_target_pairs={{2,0},{3,1},{4,2},{5,3},{6,4},{7,5},{8,6},{9,7},{10,8},{11,9},{12,... | collective-permute-start | bytes 2359304 | tf_op jit(solution)/shard_map/ppermute | solution.py:15
  30.7 6.9 %collective-permute-start.4 = (bf16[256,6,256]{0,2,1:T(8,128)(2,1)S(1)}, bf16[256,6,256]{0,2,1:T(8,128)(2,1)S(1)}, u32[]{:S(2)}, u32[]{:S(2)}) collective-permute-start(bf16[256,6,256]{0,2,1:T(8,128)(2,1)S(1)} %collective-permute-done), channel_id=1, source_target_pairs={{4,0},{5,1},{6,2},{7,3},{8,4},{9,5},{10,6},{11,7},{12,8},{13,9},{1... | collective-permute-start | bytes 2359304 | tf_op jit(solution)/shard_map/ppermute | solution.py:15
  43.3 51.5 %collective-permute-done.2 = bf16[256,6,256]{0,2,1:T(8,128)(2,1)} collective-permute-done((bf16[256,6,256]{0,2,1:T(8,128)(2,1)S(1)}, bf16[256,6,256]{0,2,1:T(8,128)(2,1)}, u32[]{:S(2)}, u32[]{:S(2)}) %collective-permute-start.2) | collective-permute-done | bytes 786464 | tf_op jit(solution)/shard_map/ppermute | solution.py:15
  96.3 69.6 %collective-permute-done.3 = bf16[256,6,256]{0,2,1:T(8,128)(2,1)S(1)} collective-permute-done((bf16[256,6,256]{0,2,1:T(8,128)(2,1)S(1)}, bf16[256,6,256]{0,2,1:T(8,128)(2,1)S(1)}, u32[]{:S(2)}, u32[]{:S(2)}) %collective-permute-start.3) | collective-permute-done | bytes 786464 | tf_op jit(solution)/shard_map/ppermute | solution.py:15
  175.2 14.9 %fusion.33 = bf16[256,6,256]{2,1,0:T(8,128)(2,1)S(1)} fusion(bf16[256,36,256]{2,0,1:T(8,128)(2,1)S(1)} %bitcast.231, bf16[1,36,36]{2,1,0:T(8,128)(2,1)S(1)} %copy-done.5), kind=kOutput, calls=%fused_computation.34 | convolution fusion | flops 28704768 | bytes 5507072 | tf_op jit(solution)/shard_map/qy,iyk->iqk/dot_general | solution.py:66
  205.9 17.8 %collective-permute-done.6 = bf16[256,6,256]{2,0,1:T(8,128)(2,1)S(1)} collective-permute-done((bf16[256,6,256]{2,0,1:T(8,128)(2,1)S(1)}, bf16[256,6,256]{2,0,1:T(8,128)(2,1)S(1)}, u32[]{:S(2)}, u32[]{:S(2)}) %collective-permute-start.6) | collective-permute-done | bytes 786464 | tf_op jit(solution)/shard_map/ppermute | solution.py:15
  224.2 75.1 %collective-permute-done.7 = bf16[256,6,256]{2,0,1:T(8,128)(2,1)S(1)} collective-permute-done((bf16[256,6,256]{2,0,1:T(8,128)(2,1)S(1)}, bf16[256,6,256]{2,0,1:T(8,128)(2,1)S(1)}, u32[]{:S(2)}, u32[]{:S(2)}) %collective-permute-start.7) | collective-permute-done | bytes 786464 | tf_op jit(solution)/shard_map/ppermute | solution.py:15
  299.7 24.9 %collective-permute-done.8 = bf16[256,6,256]{2,0,1:T(8,128)(2,1)S(1)} collective-permute-done((bf16[256,6,256]{2,0,1:T(8,128)(2,1)S(1)}, bf16[256,6,256]{2,0,1:T(8,128)(2,1)S(1)}, u32[]{:S(2)}, u32[]{:S(2)}) %collective-permute-start.8) | collective-permute-done | bytes 786464 | tf_op jit(solution)/shard_map/ppermute | solution.py:15
  326.0 4.2 copy.53
  330.1 9.5 %convolution_convert_fusion = bf16[1536,256]{1,0:T(8,128)(2,1)} fusion(bf16[1536,1536]{1,0:T(8,128)(2,1)} %bitcast.217, bf16[1,1,1536,256]{3,2,1,0:T(8,128)(2,1)S(1)} %copy-done), kind=kOutput, calls=%fused_computation.16 | convolution fusion | flops 2416705536 | bytes 6291456 | tf_op jit(solution)/shard_map/rk,rc->kc/dot_general | solution.py:22
  339.6 3.9 fusion.101
  343.6 3.7 select_reduce_fusion
  350.5 11.7 %cholesky.49 = f32[128,128]{1,0:T(8,128)S(1)} custom-call(f32[128,128]{1,0:T(8,128)S(1)} %cholesky.115), custom_call_target="Cholesky" | custom-call | tf_op jit(solution)/shard_map/jit(cholesky)/cholesky | solution.py:29
  362.3 9.8 %custom-call.15 = f32[1,128,128]{1,2,0:T(8,128)S(1)} custom-call(f32[1,128,128]{2,1,0:T(8,128)S(1)} %get-tuple-element.34), custom_call_target="InvertDiagBlocksLowerTriangular" | custom-call | tf_op jit(solution)/shard_map/jit(cholesky)/cholesky | solution.py:29
  374.3 11.9 %cholesky.103 = f32[128,128]{1,0:T(8,128)S(1)} custom-call(f32[128,128]{1,0:T(8,128)S(1)} %convolution_subtract_fusion.1), custom_call_target="Cholesky" | custom-call | tf_op jit(solution)/shard_map/jit(cholesky)/cholesky | solution.py:29
  389.3 5.3 %while.1 = (s32[]{:T(128)}, f32[256,256]{1,0:T(8,128)S(1)}, s32[2,2]{1,0:T(2,128)S(1)}, f32[2,128,128]{2,1,0:T(8,128)}, s32[]{:T(128)}) while((s32[]{:T(128)}, f32[256,256]{1,0:T(8,128)S(1)}, s32[2,2]{1,0:T(2,128)S(1)}, f32[2,128,128]{2,1,0:T(8,128)}, s32[]{:T(128)}) %tuple.35), condition=%wide.while_cond, body=%wide.while_body.sunk | while | flops 2 | bytes 132205 | solution.py:30
  394.5 20.5 %custom-call.16 = f32[2,128,128]{1,2,0:T(8,128)S(1)} custom-call(f32[2,128,128]{2,1,0:T(8,128)} %get-tuple-element.9), custom_call_target="InvertDiagBlocksLowerTriangular" | custom-call | tf_op jit(solution)/shard_map/jit(_solve_triangular)/triangular_solve | solution.py:30
  418.2 4.7 fusion.12
  425.5 24.3 %collective-permute-start.15 = (bf16[256,256]{0,1:T(8,128)(2,1)S(1)}, bf16[256,256]{0,1:T(8,128)(2,1)S(1)}, u32[]{:S(2)}, u32[]{:S(2)}) collective-permute-start(bf16[256,256]{0,1:T(8,128)(2,1)S(1)} %get-tuple-element.26), channel_id=1, source_target_pairs={{5,0},{6,1},{7,2},{8,3},{9,4},{10,5},{11,6},{12,7},{13,8},{14,9},{... | collective-permute-start | bytes 393224 | tf_op jit(solution)/shard_map/ppermute | solution.py:15
  449.8 8.6 %collective-permute-start.14 = (bf16[256,256]{0,1:T(8,128)(2,1)S(1)}, bf16[256,256]{0,1:T(8,128)(2,1)S(1)}, u32[]{:S(2)}, u32[]{:S(2)}) collective-permute-start(bf16[256,256]{0,1:T(8,128)(2,1)S(1)} %get-tuple-element.27), channel_id=1, source_target_pairs={{4,0},{5,1},{6,2},{7,3},{8,4},{9,5},{10,6},{11,7},{12,8},{13,9},{1... | collective-permute-start | bytes 393224 | tf_op jit(solution)/shard_map/ppermute | solution.py:15
  460.3 16.4 %collective-permute-start.12 = (bf16[256,256]{0,1:T(8,128)(2,1)S(1)}, bf16[256,256]{0,1:T(8,128)(2,1)S(1)}, u32[]{:S(2)}, u32[]{:S(2)}) collective-permute-start(bf16[256,256]{0,1:T(8,128)(2,1)S(1)} %get-tuple-element.29), channel_id=1, source_target_pairs={{2,0},{3,1},{4,2},{5,3},{6,4},{7,5},{8,6},{9,7},{10,8},{11,9},{12,... | collective-permute-start | bytes 393224 | tf_op jit(solution)/shard_map/ppermute | solution.py:15
  478.7 16.8 %collective-permute-done.11 = bf16[256,256]{0,1:T(8,128)(2,1)S(1)} collective-permute-done((bf16[256,256]{0,1:T(8,128)(2,1)S(1)}, bf16[256,256]{0,1:T(8,128)(2,1)S(1)}, u32[]{:S(2)}, u32[]{:S(2)}) %collective-permute-start.11) | collective-permute-done | bytes 131104 | tf_op jit(solution)/shard_map/ppermute | solution.py:15
  498.8 11.5 %collective-permute-done.16 = bf16[256,6,256]{0,2,1:T(8,128)(2,1)} collective-permute-done((bf16[256,6,256]{0,2,1:T(8,128)(2,1)}, bf16[256,6,256]{0,2,1:T(8,128)(2,1)}, u32[]{:S(2)}, u32[]{:S(2)}) %collective-permute-start.16) | collective-permute-done | bytes 786464 | tf_op jit(solution)/shard_map/ppermute | solution.py:15
  (98 shorter events, 71.2 us)
Async XLA Ops:
  0.6 329.5 %copy-start = (bf16[1,1,1536,256]{3,2,1,0:T(8,128)(2,1)S(1)}, bf16[1,1,1536,256]{3,2,1,0:T(8,128)(2,1)}, u32[]{:S(2)}) copy-start(bf16[1,1,1536,256]{3,2,1,0:T(8,128)(2,1)} %param.8) | copy-start | bytes 2359300
  0.6 41.1 %copy-start.4 = (bf16[1,1,256,6,256]{4,2,3,1,0:T(8,128)(2,1)S(1)}, bf16[1,1,256,6,256]{4,2,3,1,0:T(8,128)(2,1)}, u32[]{:S(2)}) copy-start(bf16[1,1,256,6,256]{4,2,3,1,0:T(8,128)(2,1)} %param.5) | copy-start | bytes 2359300
  2.2 11.4 %collective-permute-start = (bf16[256,6,256]{0,2,1:T(8,128)(2,1)S(1)}, bf16[256,6,256]{0,2,1:T(8,128)(2,1)S(1)}, u32[]{:S(2)}, u32[]{:S(2)}) collective-permute-start(bf16[256,6,256]{0,2,1:T(8,128)(2,1)S(1)} %bitcast.220), channel_id=1, source_target_pairs={{32,0},{64,32},{96,64},{128,96},{160,128},{192,160},{224,192},{256... | collective-permute-start | bytes 2359304 | tf_op jit(solution)/shard_map/ppermute | solution.py:15
  13.6 28.1 %collective-permute-start.1 = (bf16[256,6,256]{0,2,1:T(8,128)(2,1)S(1)}, bf16[256,6,256]{0,2,1:T(8,128)(2,1)}, u32[]{:S(2)}, u32[]{:S(2)}) collective-permute-start(bf16[256,6,256]{0,2,1:T(8,128)(2,1)S(1)} %collective-permute-done), channel_id=1, source_target_pairs={{1,0},{2,1},{3,2},{4,3},{5,4},{6,5},{7,6},{8,7},{9,8},{10,9},{11,1... | collective-permute-start | bytes 2359304 | tf_op jit(solution)/shard_map/ppermute | solution.py:15
  15.5 79.2 %collective-permute-start.2 = (bf16[256,6,256]{0,2,1:T(8,128)(2,1)S(1)}, bf16[256,6,256]{0,2,1:T(8,128)(2,1)}, u32[]{:S(2)}, u32[]{:S(2)}) collective-permute-start(bf16[256,6,256]{0,2,1:T(8,128)(2,1)S(1)} %collective-permute-done), channel_id=1, source_target_pairs={{2,0},{3,1},{4,2},{5,3},{6,4},{7,5},{8,6},{9,7},{10,8},{11,9},{12,... | collective-permute-start | bytes 2359304 | tf_op jit(solution)/shard_map/ppermute | solution.py:15
  28.7 138.0 %collective-permute-start.5 = (bf16[256,6,256]{0,2,1:T(8,128)(2,1)S(1)}, bf16[256,6,256]{0,2,1:T(8,128)(2,1)S(1)}, u32[]{:S(2)}, u32[]{:S(2)}) collective-permute-start(bf16[256,6,256]{0,2,1:T(8,128)(2,1)S(1)} %collective-permute-done), channel_id=1, source_target_pairs={{5,0},{6,1},{7,2},{8,3},{9,4},{10,5},{11,6},{12,7},{13,8},{14,9},{... | collective-permute-start | bytes 2359304 | tf_op jit(solution)/shard_map/ppermute | solution.py:15
  30.7 135.7 %collective-permute-start.4 = (bf16[256,6,256]{0,2,1:T(8,128)(2,1)S(1)}, bf16[256,6,256]{0,2,1:T(8,128)(2,1)S(1)}, u32[]{:S(2)}, u32[]{:S(2)}) collective-permute-start(bf16[256,6,256]{0,2,1:T(8,128)(2,1)S(1)} %collective-permute-done), channel_id=1, source_target_pairs={{4,0},{5,1},{6,2},{7,3},{8,4},{9,5},{10,6},{11,7},{12,8},{13,9},{1... | collective-permute-start | bytes 2359304 | tf_op jit(solution)/shard_map/ppermute | solution.py:15
  37.6 128.4 %collective-permute-start.3 = (bf16[256,6,256]{0,2,1:T(8,128)(2,1)S(1)}, bf16[256,6,256]{0,2,1:T(8,128)(2,1)S(1)}, u32[]{:S(2)}, u32[]{:S(2)}) collective-permute-start(bf16[256,6,256]{0,2,1:T(8,128)(2,1)S(1)} %collective-permute-done), channel_id=1, source_target_pairs={{3,0},{4,1},{5,2},{6,3},{7,4},{8,5},{9,6},{10,7},{11,8},{12,9},{13... | collective-permute-start | bytes 2359304 | tf_op jit(solution)/shard_map/ppermute | solution.py:15
  43.3 123.9 %copy-start.5 = (bf16[1,36,36]{2,1,0:T(8,128)(2,1)S(1)}, bf16[1,36,36]{2,1,0:T(8,128)(2,1)}, u32[]{:S(2)}) copy-start(bf16[1,36,36]{2,1,0:T(8,128)(2,1)} %param.7) | copy-start | bytes 7780
  190.3 33.4 %collective-permute-start.6 = (bf16[256,6,256]{2,0,1:T(8,128)(2,1)S(1)}, bf16[256,6,256]{2,0,1:T(8,128)(2,1)S(1)}, u32[]{:S(2)}, u32[]{:S(2)}) collective-permute-start(bf16[256,6,256]{2,0,1:T(8,128)(2,1)S(1)} %copy.32), channel_id=1, source_target_pairs={{0,1},{1,2},{2,3},{3,4},{4,5},{5,6},{6,7},{7,8},{8,9},{9,10},{10,1... | collective-permute-start | bytes 2359304 | tf_op jit(solution)/shard_map/ppermute | solution.py:15
  192.4 106.9 %collective-permute-start.7 = (bf16[256,6,256]{2,0,1:T(8,128)(2,1)S(1)}, bf16[256,6,256]{2,0,1:T(8,128)(2,1)S(1)}, u32[]{:S(2)}, u32[]{:S(2)}) collective-permute-start(bf16[256,6,256]{2,0,1:T(8,128)(2,1)S(1)} %copy.35), channel_id=1, source_target_pairs={{0,2},{1,3},{2,4},{3,5},{4,6},{5,7},{6,8},{7,9},{8,10},{9,11},{10,... | collective-permute-start | bytes 2359304 | tf_op jit(solution)/shard_map/ppermute | solution.py:15
  197.1 127.4 %collective-permute-start.8 = (bf16[256,6,256]{2,0,1:T(8,128)(2,1)S(1)}, bf16[256,6,256]{2,0,1:T(8,128)(2,1)S(1)}, u32[]{:S(2)}, u32[]{:S(2)}) collective-permute-start(bf16[256,6,256]{2,0,1:T(8,128)(2,1)S(1)} %copy.38), channel_id=1, source_target_pairs={{0,3},{1,4},{2,5},{3,6},{4,7},{5,8},{6,9},{7,10},{8,11},{9,12},{10... | collective-permute-start | bytes 2359304 | tf_op jit(solution)/shard_map/ppermute | solution.py:15
  199.2 125.8 %collective-permute-start.9 = (bf16[256,6,256]{2,0,1:T(8,128)(2,1)S(1)}, bf16[256,6,256]{2,0,1:T(8,128)(2,1)S(1)}, u32[]{:S(2)}, u32[]{:S(2)}) collective-permute-start(bf16[256,6,256]{2,0,1:T(8,128)(2,1)S(1)} %copy.41), channel_id=1, source_target_pairs={{0,4},{1,5},{2,6},{3,7},{4,8},{5,9},{6,10},{7,11},{8,12},{9,13},{1... | collective-permute-start | bytes 2359304 | tf_op jit(solution)/shard_map/ppermute | solution.py:15
  201.3 124.2 %collective-permute-start.10 = (bf16[256,6,256]{2,0,1:T(8,128)(2,1)S(1)}, bf16[256,6,256]{2,0,1:T(8,128)(2,1)S(1)}, u32[]{:S(2)}, u32[]{:S(2)}) collective-permute-start(bf16[256,6,256]{2,0,1:T(8,128)(2,1)S(1)} %copy.44), channel_id=1, source_target_pairs={{0,5},{1,6},{2,7},{3,8},{4,9},{5,10},{6,11},{7,12},{8,13},{9,14},{... | collective-permute-start | bytes 2359304 | tf_op jit(solution)/shard_map/ppermute | solution.py:15
  349.8 0.7 copy-start.3
  386.2 2.0 copy-start.2
  422.9 74.7 %copy-start.1 = (bf16[1,1,256,6,256]{2,4,3,1,0:T(8,128)(2,1)S(1)}, bf16[1,1,256,6,256]{2,4,3,1,0:T(8,128)(2,1)}, u32[]{:S(2)}) copy-start(bf16[1,1,256,6,256]{2,4,3,1,0:T(8,128)(2,1)} %copy.48) | copy-start | bytes 2359300
  425.5 72.1 %collective-permute-start.15 = (bf16[256,256]{0,1:T(8,128)(2,1)S(1)}, bf16[256,256]{0,1:T(8,128)(2,1)S(1)}, u32[]{:S(2)}, u32[]{:S(2)}) collective-permute-start(bf16[256,256]{0,1:T(8,128)(2,1)S(1)} %get-tuple-element.26), channel_id=1, source_target_pairs={{5,0},{6,1},{7,2},{8,3},{9,4},{10,5},{11,6},{12,7},{13,8},{14,9},{... | collective-permute-start | bytes 393224 | tf_op jit(solution)/shard_map/ppermute | solution.py:15
  449.8 47.8 %collective-permute-start.14 = (bf16[256,256]{0,1:T(8,128)(2,1)S(1)}, bf16[256,256]{0,1:T(8,128)(2,1)S(1)}, u32[]{:S(2)}, u32[]{:S(2)}) collective-permute-start(bf16[256,256]{0,1:T(8,128)(2,1)S(1)} %get-tuple-element.27), channel_id=1, source_target_pairs={{4,0},{5,1},{6,2},{7,3},{8,4},{9,5},{10,6},{11,7},{12,8},{13,9},{1... | collective-permute-start | bytes 393224 | tf_op jit(solution)/shard_map/ppermute | solution.py:15
  458.4 39.1 %collective-permute-start.13 = (bf16[256,256]{0,1:T(8,128)(2,1)S(1)}, bf16[256,256]{0,1:T(8,128)(2,1)S(1)}, u32[]{:S(2)}, u32[]{:S(2)}) collective-permute-start(bf16[256,256]{0,1:T(8,128)(2,1)S(1)} %get-tuple-element.28), channel_id=1, source_target_pairs={{3,0},{4,1},{5,2},{6,3},{7,4},{8,5},{9,6},{10,7},{11,8},{12,9},{13... | collective-permute-start | bytes 393224 | tf_op jit(solution)/shard_map/ppermute | solution.py:15
  460.3 37.2 %collective-permute-start.12 = (bf16[256,256]{0,1:T(8,128)(2,1)S(1)}, bf16[256,256]{0,1:T(8,128)(2,1)S(1)}, u32[]{:S(2)}, u32[]{:S(2)}) collective-permute-start(bf16[256,256]{0,1:T(8,128)(2,1)S(1)} %get-tuple-element.29), channel_id=1, source_target_pairs={{2,0},{3,1},{4,2},{5,3},{6,4},{7,5},{8,6},{9,7},{10,8},{11,9},{12,... | collective-permute-start | bytes 393224 | tf_op jit(solution)/shard_map/ppermute | solution.py:15
  476.7 18.7 %collective-permute-start.11 = (bf16[256,256]{0,1:T(8,128)(2,1)S(1)}, bf16[256,256]{0,1:T(8,128)(2,1)S(1)}, u32[]{:S(2)}, u32[]{:S(2)}) collective-permute-start(bf16[256,256]{0,1:T(8,128)(2,1)S(1)} %get-tuple-element.30), channel_id=1, source_target_pairs={{1,0},{2,1},{3,2},{4,3},{5,4},{6,5},{7,6},{8,7},{9,8},{10,9},{11,1... | collective-permute-start | bytes 393224 | tf_op jit(solution)/shard_map/ppermute | solution.py:15
  495.5 14.8 %collective-permute-start.16 = (bf16[256,6,256]{0,2,1:T(8,128)(2,1)}, bf16[256,6,256]{0,2,1:T(8,128)(2,1)}, u32[]{:S(2)}, u32[]{:S(2)}) collective-permute-start(bf16[256,6,256]{0,2,1:T(8,128)(2,1)} %bitcast.227), channel_id=1, source_target_pairs={{0,32},{32,64},{64,96},{96,128},{128,160},{160,192},{192,224},{224... | collective-permute-start | bytes 2359304 | tf_op jit(solution)/shard_map/ppermute | solution.py:15
where the time goes:
time: 517 us; the launch traced here: 513 us
  waiting for transfers between devices  276 us (53%)
  starting transfers between devices  91 us (18%)
  matrix products  61 us (12%)
  other arithmetic  58.2 us (11%)
  local copies, waits for them, and re-layouts  22.7 us (4%)
    ppermute x17, waiting for transfers between devices, shifted(): return lax.ppermute(array, axis, pairs)  276 us
    ppermute x17, starting transfers between devices, shifted(): return lax.ppermute(array, axis, pairs)  91 us
    another operation x6, other arithmetic, orthonormal_basis(): factor = jnp.linalg.cholesky(gram_matrix)  34.2 us
    dot_general x6, matrix products, per_device(): jnp.einsum('qy,iyk->iqk', gate_rows[photon], product, preferred_element_t...  28.3 us
    another operation x3, other arithmetic, orthonormal_basis(): jax.scipy.linalg.solve_triangular(factor, sketch.T, lower=True)  21.5 us
    unnamed x26, local copies, waits for them, and re-layouts  12.9 us
  transfers between devices with their start and end apart: 17, of which 8 were waited for; matrix products, arithmetic and copies ran while one was open for 3% of the time, Pallas kernels for 0%

commit v1 on v0

v1 whole, which is shorter than its diff:
```python
import functools
import math

import jax
import jax.numpy as jnp
from jax import lax
from jax.experimental import pallas as pl
from jax.experimental.pallas import tpu as pltpu
from jax.sharding import PartitionSpec as P

RIDGE_SHARE = 0.05
TINY_SHIFT = 1e-05
MESH = pl.DeviceIdType.MESH
HIGHEST = lax.Precision.HIGHEST
VMEM_LIMIT = 48 * 1024 * 1024


def ring(index, by, size):
    return lax.rem(index + (by + size), size)


def greet(partners):
    barrier = pltpu.get_barrier_semaphore()
    for partner in partners:
        pl.semaphore_signal(barrier, inc=1, device_id=partner, device_id_type=MESH)
    pl.semaphore_wait(barrier, len(partners))


def gather_kernel(
    levels, chains, sectors,
    gate_ref, left_ref, right_ref, block_ref,
    left_in, right_in,
    chain_send, chain_recv, left_send, left_recv, up_send, up_recv, down_send, down_recv,
):
    chain, sector = lax.axis_index("chain"), lax.axis_index("sector")
    above = (chain, ring(sector, 1, sectors))
    below = (chain, ring(sector, -1, sectors))
    before = (ring(chain, -1, chains), sector)
    after = (ring(chain, 1, chains), sector)
    greet((above, below, before, after))
    last = levels - 1
    size = left_ref.shape[1]

    def slot(offset, r):
        return right_in.at[r + offset, last - r]

    def chain_copy(r):
        return pltpu.make_async_remote_copy(
            src_ref=right_ref.at[r], dst_ref=slot(0, r), send_sem=chain_send.at[r], recv_sem=chain_recv.at[r],
            device_id=before, device_id_type=MESH,
        )

    def left_copy(hop, n):
        source = left_ref.at[n] if hop == 1 else left_in.at[hop - 2, n]
        return pltpu.make_async_remote_copy(
            src_ref=source, dst_ref=left_in.at[hop - 1, n], send_sem=left_send.at[hop - 1, n],
            recv_sem=left_recv.at[hop - 1, n], device_id=above, device_id_type=MESH,
        )

    def up_copy(hop, r):
        return pltpu.make_async_remote_copy(
            src_ref=slot(1 - hop, r), dst_ref=slot(-hop, r), send_sem=up_send.at[hop - 1, r],
            recv_sem=up_recv.at[hop - 1, r], device_id=above, device_id_type=MESH,
        )

    def down_copy(hop, r):
        return pltpu.make_async_remote_copy(
            src_ref=slot(hop - 1, r), dst_ref=slot(hop, r), send_sem=down_send.at[hop - 1, r],
            recv_sem=down_recv.at[hop - 1, r], device_id=below, device_id_type=MESH,
        )

    def build_row(p):
        source = left_ref if p == 0 else left_in.at[p - 1]
        for q in range(levels):
            value = None
            for n in range(levels):
                r = p + q - n
                if 0 <= r <= last:
                    product = jnp.dot(source[n], right_in[q, last - r], preferred_element_type=jnp.float32)
                    product = product.astype(jnp.bfloat16).astype(jnp.float32)
                    term = product * gate_ref[(p * levels + q) * levels + n]
                    value = term if value is None else value + term
            block_ref[p * size:(p + 1) * size, q * size:(q + 1) * size] = value.astype(jnp.bfloat16)

    for r in range(levels):
        chain_copy(r).start()
    for n in range(levels):
        left_copy(1, n).start()
    for r in range(levels):
        chain_copy(r).wait_recv()
        if r < last:
            down_copy(1, r).start()
        if r > 0:
            up_copy(1, r).start()
    for hop in range(1, levels):
        for r in range(levels):
            if r + hop <= last:
                down_copy(hop, r).wait_recv()
                if r + hop < last:
                    down_copy(hop + 1, r).start()
            if r >= hop:
                up_copy(hop, r).wait_recv()
                if r > hop:
                    up_copy(hop + 1, r).start()
        for n in range(levels):
            left_copy(hop, n).wait_recv()
            if hop < last:
                left_copy(hop + 1, n).start()
        for p in range(levels):
            if max(p, last - p) == hop:
                build_row(p)
    for r in range(levels):
        chain_copy(r).wait_send()
    for hop in range(1, levels):
        for r in range(levels):
            left_copy(hop, r).wait_send()
            if r + hop <= last:
                down_copy(hop, r).wait_send()
            if r >= hop:
                up_copy(hop, r).wait_send()


def gather_blocks(gates, left, right, chains, sectors):
    levels, size = left.shape[0], left.shape[1]
    hops = pltpu.SemaphoreType.DMA((levels - 1, levels))
    one = pltpu.SemaphoreType.DMA((levels,))
    return pl.pallas_call(
        functools.partial(gather_kernel, levels, chains, sectors),
        out_shape=jax.ShapeDtypeStruct((levels * size, levels * size), jnp.bfloat16),
        in_specs=[
            pl.BlockSpec(memory_space=pltpu.SMEM),
            pl.BlockSpec(memory_space=pltpu.VMEM),
            pl.BlockSpec(memory_space=pl.ANY),
        ],
        out_specs=pl.BlockSpec(memory_space=pltpu.VMEM),
        scratch_shapes=[
            pltpu.VMEM((levels - 1, levels, size, size), jnp.bfloat16),
            pltpu.VMEM((levels, levels, size, size), jnp.bfloat16),
            one, one, hops, hops, hops, hops, hops, hops,
        ],
        compiler_params=pltpu.CompilerParams(
            collective_id=0, has_side_effects=True, vmem_limit_bytes=VMEM_LIMIT
        ),
    )(gates, left, right)


def scatter_kernel(
    levels, chains, sectors,
    pieces_ref, right_ref, left_out, right_out,
    own_sem, chain_send, chain_recv, send, recv,
):
    chain, sector = lax.axis_index("chain"), lax.axis_index("sector")
    before = (ring(chain, -1, chains), sector)
    after = (ring(chain, 1, chains), sector)
    below = [(chain, ring(sector, -p, sectors)) for p in range(1, levels)]
    above = [(chain, ring(sector, p, sectors)) for p in range(1, levels)]
    greet((before, after, *below, *above))
    own = pltpu.make_async_copy(pieces_ref.at[0], left_out.at[0], own_sem)
    chain_copy = pltpu.make_async_remote_copy(
        src_ref=right_ref, dst_ref=right_out, send_sem=chain_send, recv_sem=chain_recv,
        device_id=after, device_id_type=MESH,
    )
    copies = [
        pltpu.make_async_remote_copy(
            src_ref=pieces_ref.at[p], dst_ref=left_out.at[p], send_sem=send.at[p - 1], recv_sem=recv.at[p - 1],
            device_id=below[p - 1], device_id_type=MESH,
        )
        for p in range(1, levels)
    ]
    for copy in reversed(copies):
        copy.start()
    chain_copy.start()
    own.start()
    own.wait()
    for copy in copies:
        copy.wait()
    chain_copy.wait()


def scatter(pieces, fresh_right, chains, sectors):
    levels = pieces.shape[0]
    return pl.pallas_call(
        functools.partial(scatter_kernel, levels, chains, sectors),
        out_shape=(
            jax.ShapeDtypeStruct(pieces.shape, pieces.dtype),
            jax.ShapeDtypeStruct(fresh_right.shape, fresh_right.dtype),
        ),
        in_specs=[pl.BlockSpec(memory_space=pl.ANY)] * 2,
        out_specs=(pl.BlockSpec(memory_space=pl.ANY),) * 2,
        scratch_shapes=[
            pltpu.SemaphoreType.DMA,
            pltpu.SemaphoreType.DMA,
            pltpu.SemaphoreType.DMA,
            pltpu.SemaphoreType.DMA((levels - 1,)),
            pltpu.SemaphoreType.DMA((levels - 1,)),
        ],
        compiler_params=pltpu.CompilerParams(collective_id=1, has_side_effects=True),
    )(pieces, fresh_right)


def sketch_kernel(block_ref, test_ref, sketch_ref, gram_ref):
    contract_rows = (((0,), (0,)), ((), ()))
    contract_columns = (((1,), (1,)), ((), ()))
    block = block_ref[...]
    first = jnp.dot(block, test_ref[...], preferred_element_type=jnp.float32).astype(jnp.bfloat16)
    back = lax.dot_general(first, block, contract_rows, preferred_element_type=jnp.float32).astype(jnp.bfloat16)
    sketch = lax.dot_general(block, back, contract_columns, preferred_element_type=jnp.float32)
    sketch_ref[...] = sketch
    size = sketch.shape[1]
    gram = lax.dot_general(sketch, sketch, contract_rows, precision=HIGHEST, preferred_element_type=jnp.float32)
    diagonal = lax.broadcasted_iota(jnp.int32, (size, size), 0) == lax.broadcasted_iota(jnp.int32, (size, size), 1)
    trace = jnp.sum(jnp.where(diagonal, gram, 0.0))
    gram_ref[...] = gram + jnp.where(diagonal, RIDGE_SHARE * trace / size + TINY_SHIFT, 0.0)


def make_sketch(block, test_matrix):
    rows, size = test_matrix.shape
    return pl.pallas_call(
        sketch_kernel,
        out_shape=(
            jax.ShapeDtypeStruct((rows, size), jnp.float32),
            jax.ShapeDtypeStruct((size, size), jnp.float32),
        ),
        in_specs=[pl.BlockSpec(memory_space=pltpu.VMEM)] * 2,
        out_specs=(pl.BlockSpec(memory_space=pltpu.VMEM),) * 2,
        compiler_params=pltpu.CompilerParams(vmem_limit_bytes=VMEM_LIMIT),
    )(block, test_matrix)


def inverse_factor_kernel(width, gram_ref, inverse_ref, work):
    size = gram_ref.shape[0]
    contract_rows = (((0,), (0,)), ((), ()))

    def iota(shape, dim):
        return lax.broadcasted_iota(jnp.int32, shape, dim)

    work[:, :size] = gram_ref[...]
    work[:, size:] = jnp.where(iota((size, size), 0) == iota((size, size), 1), 1.0, 0.0)
    for start in range(0, size, width):
        stop = start + width
        eye = jnp.where(iota((width, width), 0) == iota((width, width), 1), 1.0, 0.0)
        local = jnp.concatenate([work[start:stop, start:stop], eye], axis=1)
        rows = [local[8 * t:8 * (t + 1)] for t in range(width // 8)]
        index = iota((8, 2 * width), 0)
        for k in range(0, width, 2):
            t0, s = k // 8, k % 8
            tile = rows[t0]
            row0 = tile[s:s + 1]
            row1 = tile[s + 1:s + 2]
            a = row0[:, k:k + 1]
            b = row0[:, k + 1:k + 2]
            c = row1[:, k + 1:k + 2]
            inv_a = 1.0 / a
            ratio = b * inv_a
            inv_c = 1.0 / (c - b * ratio)
            row1 = row1 - ratio * row0
            scaled0 = row0 * inv_a
            scaled1 = row1 * inv_c
            for t in range(t0, width // 8):
                m0 = rows[t][:, k:k + 1]
                m1 = rows[t][:, k + 1:k + 2] - m0 * ratio
                updated = rows[t] - m0 * scaled0 - m1 * scaled1
                if t == t0:
                    keep = jnp.where(index == s + 1, row1, rows[t])
                    updated = jnp.where(index > s + 1, updated, keep)
                rows[t] = updated
        reduced = jnp.concatenate(rows, axis=0)
        pivots = jnp.sum(reduced[:, :width] * eye, axis=1, keepdims=True)
        small = reduced[:, width:] * lax.rsqrt(pivots)
        top = jnp.dot(small, work[start:stop, :], precision=HIGHEST, preferred_element_type=jnp.float32)
        inverse_ref[start:stop, :] = top[:, size:]
        if stop < size:
            work[stop:, :] -= lax.dot_general(
                top[:, stop:size], top, contract_rows, precision=HIGHEST, preferred_element_type=jnp.float32
            )


def inverse_factor(gram):
    size = gram.shape[0]
    return pl.pallas_call(
        functools.partial(inverse_factor_kernel, min(64, size)),
        out_shape=jax.ShapeDtypeStruct((size, size), jnp.float32),
        in_specs=[pl.BlockSpec(memory_space=pltpu.VMEM)],
        out_specs=pl.BlockSpec(memory_space=pltpu.VMEM),
        scratch_shapes=[pltpu.VMEM((size, 2 * size), jnp.float32)],
        compiler_params=pltpu.CompilerParams(vmem_limit_bytes=VMEM_LIMIT),
    )(gram)


def basis_kernel(scale, kept_ref, block_ref, sketch_ref, inverse_ref, pieces_ref, right_ref):
    contract_rows = (((0,), (0,)), ((), ()))
    contract_columns = (((1,), (1,)), ((), ()))
    basis = lax.dot_general(
        sketch_ref[...], inverse_ref[...], contract_columns, precision=HIGHEST, preferred_element_type=jnp.float32
    )
    column = lax.broadcasted_iota(jnp.int32, basis.shape, 1)
    scaled = (jnp.where(column < kept_ref[0], basis, 0.0) * scale).astype(jnp.bfloat16)
    pieces_ref[...] = scaled
    fresh = lax.dot_general(scaled, block_ref[...], contract_rows, preferred_element_type=jnp.float32)
    fresh = fresh * (1.0 / scale)
    levels, size = right_ref.shape[0], right_ref.shape[1]
    for q in range(levels):
        right_ref[q] = fresh[:, q * size:(q + 1) * size].astype(jnp.bfloat16)


def make_basis(kept, block, sketch, inverse, levels):
    rows, size = sketch.shape
    return pl.pallas_call(
        functools.partial(basis_kernel, math.sqrt(rows)),
        out_shape=(
            jax.ShapeDtypeStruct((rows, size), jnp.bfloat16),
            jax.ShapeDtypeStruct((levels, size, size), jnp.bfloat16),
        ),
        in_specs=[pl.BlockSpec(memory_space=pltpu.SMEM)] + [pl.BlockSpec(memory_space=pltpu.VMEM)] * 3,
        out_specs=(pl.BlockSpec(memory_space=pltpu.VMEM),) * 2,
        compiler_params=pltpu.CompilerParams(vmem_limit_bytes=VMEM_LIMIT),
    )(kept, block, sketch, inverse)


def level_gates(gates, levels, sector, sectors):
    p = jnp.arange(levels)[:, None, None]
    q = jnp.arange(levels)[None, :, None]
    n = jnp.arange(levels)[None, None, :]
    r = p + q - n
    inside = (r >= 0) & (r < levels)
    r = jnp.clip(r, 0, levels - 1)
    chosen = gates.astype(jnp.float32)[p * levels + q, n * levels + r]
    inside = inside & (sector - p >= 0) & (sector + q < sectors)
    return jnp.where(inside, chosen, 0.0).reshape(-1)


def per_device(left_sites, right_sites, pair_gates, test_matrix, kept_columns):
    levels = left_sites.shape[3]
    size = left_sites.shape[2]
    sectors = lax.axis_size("sector")
    sector = lax.axis_index("sector")
    chains = lax.axis_size("chain")
    chain = lax.axis_index("chain")
    left = jnp.transpose(left_sites[0, 0], (1, 0, 2))
    right = jnp.transpose(right_sites[0, 0], (1, 0, 2))
    gates = level_gates(pair_gates[0], levels, sector, sectors)
    block = gather_blocks(gates, left, right, chains, sectors)
    sketch, gram = make_sketch(block, test_matrix[0, 0])
    inverse = inverse_factor(gram)
    pieces, fresh_right = make_basis(kept_columns[0], block, sketch, inverse, levels)
    fresh_left, shipped = scatter(pieces.reshape(levels, size, size), fresh_right, chains, sectors)
    inside = sector + jnp.arange(levels)[:, None, None] < sectors
    fresh_left = jnp.where(inside, fresh_left, jnp.zeros_like(fresh_left))
    new_left = jnp.where(chain == chains - 1, left, fresh_left)
    new_right = jnp.where(chain == 0, right, shipped)
    return (
        jnp.transpose(new_left, (1, 0, 2))[None, None],
        jnp.transpose(new_right, (1, 0, 2))[None, None],
    )


def solution(mesh):
    return jax.shard_map(
        per_device,
        mesh=mesh,
        in_specs=(
            P("chain", "sector", None, None, None),
            P("chain", "sector", None, None, None),
            P("chain", None, None),
            P("chain", "sector", None, None),
            P("chain", "sector"),
        ),
        out_specs=(P("chain", "sector", None, None, None), P("chain", "sector", None, None, None)),
        check_vma=False,
    )
```

time: 517 us -> 243 us (0.47)
  the two profiles are of different devices: /device:TPU:102 before, /device:TPU:1 now
where the time goes in v1:
time: 243 us; the launch traced here: 241 us
  Pallas kernels  230 us (95%)
  other arithmetic  5.22 us (2%)
  local copies, waits for them, and re-layouts  4.85 us (2%)
    pallas_call x1, Pallas kernels, gather_blocks(): pl.pallas_call(functools.partial(gather_kernel, levels, chains, sectors),...  146 us
    pallas_call x1, Pallas kernels, inverse_factor(): pl.pallas_call(functools.partial(inverse_factor_kernel, min(64, size)), o...  38.7 us
    pallas_call x1, Pallas kernels, scatter(): pl.pallas_call(functools.partial(scatter_kernel, levels, chains, sectors)...  27.2 us
    pallas_call x1, Pallas kernels, make_sketch(): pl.pallas_call(sketch_kernel, out_shape=(jax.ShapeDtypeStruct((rows, size...  10.3 us
    pallas_call x1, Pallas kernels, make_basis(): pl.pallas_call(functools.partial(basis_kernel, math.sqrt(rows)), out_shap...  7.2 us

profile of v1, /device:TPU:1, one launch (start us, length us, event | category | flops | bytes accessed | tf_op | source)
XLA Modules:
  0.0 241.1 jit_solution(7940510632648763596)
XLA Ops:
  0.6 0.1 fusion.10
  0.7 0.1 fusion.2
  0.8 0.1 reshape.127
  0.9 0.7 bitcast_convert_fusion
  1.6 0.0 copy-start
  1.6 0.0 copy-start.1
  1.6 2.8 %gather_fusion = f32[216]{0:T(256)S(1)} fusion(f32[36,36]{1,0:T(8,128)S(1)} %bitcast_convert_fusion, s32[216]{0:T(256)S(1)} %reshape.127), kind=kCustom, calls=%fused_computation | custom fusion | bytes 3456 | tf_op jit(solution)/shard_map/gather | solution.py:327
  4.4 0.0 copy-start.4
  4.4 0.1 reshape.130
  4.5 0.1 fusion.8
  4.6 0.1 reshape.126.gate_ref
  4.7 0.0 copy-done
  4.7 0.0 copy-done.1
  4.8 146.1 %shard_map.68.block_ref = bf16[1536,1536]{1,0:T(8,128)(2,1)} custom-call(f32[216]{0:T(256)S(1)} %reshape.126.gate_ref, bf16[6,256,256]{2,1,0:T(8,128)(2,1)S(1)} %bitcast.26, bf16[6,256,256]{2,1,0:T(8,128)(2,1)S(1)} %bitcast.25), custom_call_target="tpu_custom_call" | custom-call | tf_op jit(solution)/shard_map/pallas_call | solution.py:127
  150.9 0.0 copy-done.4
  150.9 10.3 %shard_map.69 = (f32[1536,256]{1,0:T(8,128)S(1)}, f32[256,256]{1,0:T(8,128)S(1)}) custom-call(bf16[1536,1536]{1,0:T(8,128)(2,1)} %shard_map.68.block_ref, bf16[1536,256]{1,0:T(8,128)(2,1)S(1)} %bitcast.28), custom_call_target="tpu_custom_call" | custom-call | tf_op jit(solution)/shard_map/pallas_call | solution.py:218
  161.2 38.7 %shard_map.70.inverse_ref = f32[256,256]{1,0:T(8,128)S(1)} custom-call(f32[256,256]{1,0:T(8,128)S(1)} %get-tuple-element.9.gram_ref), custom_call_target="tpu_custom_call" | custom-call | tf_op jit(solution)/shard_map/pallas_call | solution.py:280
  200.6 7.2 %shard_map.71 = (bf16[1536,256]{1,0:T(8,128)(2,1)S(1)}, bf16[6,256,256]{2,1,0:T(8,128)(2,1)S(1)}) custom-call(s32[1]{0:T(128)} %bitcast.24.kept_ref, bf16[1536,1536]{1,0:T(8,128)(2,1)} %shard_map.68.block_ref, f32[1536,256]{1,0:T(8,128)S(1)} %get-tuple-element.8.sketch_ref, f32[256,256]{1,0:T(8,128)S(1)} %shard_map.70.inverse_ref), custom_call_target="tpu_custom_call" | custom-call | tf_op jit(solution)/shard_map/pallas_call | solution.py:308
  207.8 0.0 copy-start.2
  207.8 0.9 copy-done.2
  208.7 0.9 copy-done.3
  209.5 27.2 %shard_map.72 = (bf16[6,256,256]{2,1,0:T(8,128)(2,1)}, bf16[6,256,256]{2,1,0:T(8,128)(2,1)}) custom-call(bf16[6,256,256]{2,1,0:T(8,128)(2,1)} %bitcast.27, bf16[6,256,256]{2,1,0:T(8,128)(2,1)} %copy-done.3), custom_call_target="tpu_custom_call" | custom-call | tf_op jit(solution)/shard_map/pallas_call | solution.py:182
  236.8 2.1 select_bitcast_fusion
  238.9 2.2 select_bitcast_fusion.1
  (3 shorter events, 0.0 us)
Async XLA Ops:
  1.6 3.1 %copy-start = (bf16[1,1,256,6,256]{4,2,3,1,0:T(8,128)(2,1)S(1)}, bf16[1,1,256,6,256]{4,2,3,1,0:T(8,128)(2,1)}, u32[]{:S(2)}) copy-start(bf16[1,1,256,6,256]{4,2,3,1,0:T(8,128)(2,1)} %param.6) | copy-start | bytes 2359300
  1.6 3.1 %copy-start.1 = (bf16[1,1,256,6,256]{4,2,3,1,0:T(8,128)(2,1)S(1)}, bf16[1,1,256,6,256]{4,2,3,1,0:T(8,128)(2,1)}, u32[]{:S(2)}) copy-start(bf16[1,1,256,6,256]{4,2,3,1,0:T(8,128)(2,1)} %param.5) | copy-start | bytes 2359300
  4.4 146.5 %copy-start.4 = (bf16[1,1,1536,256]{3,2,1,0:T(8,128)(2,1)S(1)}, bf16[1,1,1536,256]{3,2,1,0:T(8,128)(2,1)}, u32[]{:S(2)}) copy-start(bf16[1,1,1536,256]{3,2,1,0:T(8,128)(2,1)} %param.8) | copy-start | bytes 2359300
  207.8 0.9 copy-start.2
  208.7 0.9 copy-start.3

commit v2 on v0

v2 whole, which is shorter than its diff:
```python
import functools
import math

import jax
import jax.numpy as jnp
from jax import lax
from jax.experimental import pallas as pl
from jax.experimental.pallas import tpu as pltpu
from jax.sharding import PartitionSpec as P

RIDGE_SHARE = 0.05
TINY_SHIFT = 1e-05
MESH = pl.DeviceIdType.MESH
HIGHEST = lax.Precision.HIGHEST
VMEM_LIMIT = 56 * 1024 * 1024
ROWS = (((0,), (0,)), ((), ()))
COLUMNS = (((1,), (1,)), ((), ()))


def ring(index, by, size):
    return lax.rem(index + (by + size), size)


def iota(shape, dim):
    return lax.broadcasted_iota(jnp.int32, shape, dim)


def identity(size):
    return jnp.where(iota((size, size), 0) == iota((size, size), 1), 1.0, 0.0)


def eliminate(local, width):
    shape = (8, 2 * width)
    tiles = [local[8 * t:8 * (t + 1)] for t in range(width // 8)]
    index = iota(shape, 0)
    for t0 in range(width // 8):
        columns = [
            [jnp.broadcast_to(tile[:, 8 * t0 + j:8 * t0 + j + 1], shape) for tile in tiles[t0:]] for j in range(8)
        ]
        rows = [jnp.broadcast_to(tiles[t0][j:j + 1], shape) for j in range(8)]
        pivots = [[jnp.broadcast_to(columns[l][0][j:j + 1], shape) for l in range(j + 1)] for j in range(8)]
        scaled = []
        for j in range(8):
            inverse = 1.0 / pivots[j][j]
            for i in range(j + 1, 8):
                share = pivots[i][j] * inverse
                for l in range(j + 1, i + 1):
                    pivots[i][l] = pivots[i][l] - share * pivots[l][j]
                rows[i] = rows[i] - share * rows[j]
                columns[i] = [x - share * y for x, y in zip(columns[i], columns[j])]
            scaled.append(rows[j] * inverse)
        kept = tiles[t0]
        for j in range(1, 8):
            kept = jnp.where(index == j, rows[j], kept)
        tiles[t0] = kept
        for t in range(t0 + 1, width // 8):
            for j in range(8):
                tiles[t] = tiles[t] - columns[j][t - t0] * scaled[j]
    return jnp.concatenate(tiles, axis=0)


def invert_factor(width, work):
    size = work.shape[0]
    for start in range(0, size, width):
        stop = start + width
        eye = identity(width)
        reduced = eliminate(jnp.concatenate([work[start:stop, start:stop], eye], axis=1), width)
        pivots = jnp.sum(reduced[:, :width] * eye, axis=1, keepdims=True)
        small = reduced[:, width:] * lax.rsqrt(pivots)
        top = jnp.dot(small, work[start:stop, :], precision=HIGHEST, preferred_element_type=jnp.float32)
        work[start:stop, size:] = top[:, size:]
        if stop < size:
            work[stop:, :] -= lax.dot_general(
                top[:, stop:size], top, ROWS, precision=HIGHEST, preferred_element_type=jnp.float32
            )


def layer_kernel(
    levels, chains, sectors,
    gate_ref, kept_ref, left_ref, test_ref, right_ref,
    left_out, right_out,
    left_in, right_in, total, block, back_total, sketch, work, pieces, fresh,
    chain_send, chain_recv, left_send, left_recv, far_send, far_recv, up_send, up_recv, down_send, down_recv,
    piece_send, piece_recv, fresh_send, fresh_recv, own_sem,
):
    chain, sector = lax.axis_index("chain"), lax.axis_index("sector")
    above = [(chain, ring(sector, p, sectors)) for p in range(levels)]
    below = [(chain, ring(sector, -p, sectors)) for p in range(levels)]
    before = (ring(chain, -1, chains), sector)
    after = (ring(chain, 1, chains), sector)
    partners = (before, after, *above[1:], *below[1:])
    last = levels - 1
    size = left_ref.shape[1]
    near = last - 2
    turned = levels // 2

    def remote(source, target, send_sem, recv_sem, device):
        return pltpu.make_async_remote_copy(
            src_ref=source, dst_ref=target, send_sem=send_sem, recv_sem=recv_sem, device_id=device, device_id_type=MESH
        )

    def slot(offset, r):
        return right_in.at[r + offset, last - r]

    def chain_copy(r):
        return remote(right_ref.at[r], slot(0, r), chain_send.at[r], chain_recv.at[r], before)

    def left_copy(hop, n):
        sems = left_send.at[hop - 1, n], left_recv.at[hop - 1, n]
        if hop == near + 1 and n < turned:
            return remote(left_in.at[last - 1, n], left_in.at[hop - 1, n], *sems, below[1])
        source = left_ref.at[n] if hop == 1 else left_in.at[hop - 2, n]
        return remote(source, left_in.at[hop - 1, n], *sems, above[1])

    def far_copy(n):
        return remote(left_ref.at[n], left_in.at[last - 1, n], far_send.at[n], far_recv.at[n], above[last])

    def up_copy(hop, r):
        return remote(slot(1 - hop, r), slot(-hop, r), up_send.at[hop - 1, r], up_recv.at[hop - 1, r], above[1])

    def down_copy(hop, r):
        return remote(slot(hop - 1, r), slot(hop, r), down_send.at[hop - 1, r], down_recv.at[hop - 1, r], below[1])

    def piece_copy(p):
        return remote(pieces.at[p], left_out.at[p], piece_send.at[p - 1], piece_recv.at[p - 1], below[p])

    def fresh_copy(q):
        return remote(fresh.at[q], right_out.at[q], fresh_send.at[q], fresh_recv.at[q], after)

    def gate(p, q, n):
        inside = (sector >= p) & (sector + q < sectors)
        return jnp.where(inside, gate_ref[p * levels + q, n * levels + p + q - n], 0.0)

    def add_term(p, n):
        source = left_ref.at[n] if p == 0 else left_in.at[p - 1, n]
        for q in range(levels):
            r = p + q - n
            if 0 <= r <= last:
                product = jnp.dot(source[...], right_in[q, last - r], preferred_element_type=jnp.float32)
                term = product.astype(jnp.bfloat16).astype(jnp.float32) * gate(p, q, n)
                if n == max(0, p + q - last):
                    total[p, q] = term
                else:
                    total[p, q] += term

    def finish_row(p):
        for q in range(levels):
            block[p * size:(p + 1) * size, q * size:(q + 1) * size] = total[p, q].astype(jnp.bfloat16)
        row = block[p * size:(p + 1) * size, :]
        first = jnp.dot(row, test_ref[...], preferred_element_type=jnp.float32).astype(jnp.bfloat16)
        back_total[...] += lax.dot_general(first, row, ROWS, preferred_element_type=jnp.float32)

    barrier = pltpu.get_barrier_semaphore()
    for partner in partners:
        pl.semaphore_signal(barrier, inc=1, device_id=partner, device_id_type=MESH)
    pl.semaphore_wait(barrier, len(partners))

    queue = []

    def ready(hop):
        for p in range(min(hop, near) + 1):
            for n in range(levels):
                if max(p, abs(n - p)) == hop:
                    queue.append(functools.partial(add_term, p, n))
                    if n == last:
                        queue.append(functools.partial(finish_row, p))

    def work_on(count):
        for _ in range(min(count, len(queue))):
            queue.pop(0)()

    for r in range(levels):
        chain_copy(r).start()
    for n in range(levels):
        left_copy(1, n).start()
    for n in range(levels):
        far_copy(n).start()
    back_total[...] = jnp.zeros_like(back_total)
    for r in range(levels):
        chain_copy(r).wait_recv()
        if r < last:
            down_copy(1, r).start()
        if r > 0:
            up_copy(1, r).start()
    ready(0)
    for hop in range(1, levels):
        for n in range(levels):
            if hop <= near:
                left_copy(hop, n).wait_recv()
                if hop < near or n >= turned:
                    left_copy(hop + 1, n).start()
            if n >= hop:
                up_copy(hop, n).wait_recv()
                if n > hop:
                    up_copy(hop + 1, n).start()
            if n + hop <= last:
                down_copy(hop, n).wait_recv()
                if n + hop < last:
                    down_copy(hop + 1, n).start()
            work_on(2)
        if hop == 2:
            for n in range(turned):
                far_copy(n).wait_recv()
                left_copy(near + 1, n).start()
        ready(hop)
    work_on(len(queue))
    for p in range(near + 1, levels):
        for n in range(levels):
            if p < last:
                left_copy(p, n).wait_recv()
            elif n >= turned:
                far_copy(n).wait_recv()
            add_term(p, n)
        finish_row(p)

    back = back_total[...].astype(jnp.bfloat16)
    sketch[...] = lax.dot_general(block[...], back, COLUMNS, preferred_element_type=jnp.float32)
    gram = lax.dot_general(sketch[...], sketch[...], ROWS, precision=HIGHEST, preferred_element_type=jnp.float32)
    eye = identity(size)
    ridge = RIDGE_SHARE * jnp.sum(gram * eye) / size + TINY_SHIFT
    work[:, :size] = gram + ridge * eye
    work[:, size:] = eye
    invert_factor(min(64, size), work)
    basis = lax.dot_general(sketch[...], work[:, size:], COLUMNS, precision=HIGHEST, preferred_element_type=jnp.float32)
    scale = math.sqrt(levels * size)
    scaled = jnp.where(iota(basis.shape, 1) < kept_ref[0, 0], basis, 0.0) * scale
    scaled = scaled.astype(jnp.bfloat16)
    for p in range(levels):
        pieces[p] = scaled[p * size:(p + 1) * size]
    for p in range(last, 0, -1):
        piece_copy(p).start()
    own_copy = pltpu.make_async_copy(pieces.at[0], left_out.at[0], own_sem)
    own_copy.start()
    new_right = lax.dot_general(scaled, block[...], ROWS, preferred_element_type=jnp.float32) * (1.0 / scale)
    for q in range(levels):
        fresh[q] = new_right[:, q * size:(q + 1) * size].astype(jnp.bfloat16)
        fresh_copy(q).start()
    for r in range(levels):
        chain_copy(r).wait_send()
        far_copy(r).wait_send()
    for hop in range(1, levels):
        for r in range(levels):
            if hop < last:
                left_copy(hop, r).wait_send()
            if r + hop <= last:
                down_copy(hop, r).wait_send()
            if r >= hop:
                up_copy(hop, r).wait_send()
    own_copy.wait()
    for q in range(levels):
        fresh_copy(q).wait()
    for p in range(1, levels):
        piece_copy(p).wait()


def run_layer(gates, kept, left, right, test_matrix, chains, sectors):
    levels, size = left.shape[0], left.shape[1]
    hops = pltpu.SemaphoreType.DMA((levels - 1, levels))
    one = pltpu.SemaphoreType.DMA((levels,))
    part = (levels, size, size)
    return pl.pallas_call(
        functools.partial(layer_kernel, levels, chains, sectors),
        out_shape=(jax.ShapeDtypeStruct(part, jnp.bfloat16), jax.ShapeDtypeStruct(part, jnp.bfloat16)),
        in_specs=[
            pl.BlockSpec(memory_space=pltpu.SMEM),
            pl.BlockSpec(memory_space=pltpu.SMEM),
            pl.BlockSpec(memory_space=pltpu.VMEM),
            pl.BlockSpec(memory_space=pltpu.VMEM),
            pl.BlockSpec(memory_space=pl.ANY),
        ],
        out_specs=(pl.BlockSpec(memory_space=pl.ANY),) * 2,
        scratch_shapes=[
            pltpu.VMEM((levels - 1, *part), jnp.bfloat16),
            pltpu.VMEM((levels, *part), jnp.bfloat16),
            pltpu.VMEM((levels, *part), jnp.float32),
            pltpu.VMEM((levels * size, levels * size), jnp.bfloat16),
            pltpu.VMEM((size, levels * size), jnp.float32),
            pltpu.VMEM((levels * size, size), jnp.float32),
            pltpu.VMEM((size, 2 * size), jnp.float32),
            pltpu.VMEM(part, jnp.bfloat16),
            pltpu.VMEM(part, jnp.bfloat16),
            one, one, hops, hops, one, one, hops, hops, hops, hops, one, one, one, one,
            pltpu.SemaphoreType.DMA,
        ],
        compiler_params=pltpu.CompilerParams(
            collective_id=0, has_side_effects=True, vmem_limit_bytes=VMEM_LIMIT
        ),
    )(gates, kept, left, test_matrix, right)


def per_device(left_sites, right_sites, pair_gates, test_matrix, kept_columns):
    levels = left_sites.shape[3]
    sectors = lax.axis_size("sector")
    sector = lax.axis_index("sector")
    chains = lax.axis_size("chain")
    chain = lax.axis_index("chain")
    left = jnp.transpose(left_sites[0, 0], (1, 0, 2))
    right = jnp.transpose(right_sites[0, 0], (1, 0, 2))
    gates = pair_gates[0].astype(jnp.float32)
    fresh_left, shipped = run_layer(gates, kept_columns, left, right, test_matrix[0, 0], chains, sectors)
    inside = sector + jnp.arange(levels)[:, None, None] < sectors
    fresh_left = jnp.where(inside, fresh_left, jnp.zeros_like(fresh_left))
    new_left = jnp.where(chain == chains - 1, left, fresh_left)
    new_right = jnp.where(chain == 0, right, shipped)
    return (
        jnp.transpose(new_left, (1, 0, 2))[None, None],
        jnp.transpose(new_right, (1, 0, 2))[None, None],
    )


def solution(mesh):
    return jax.shard_map(
        per_device,
        mesh=mesh,
        in_specs=(
            P("chain", "sector", None, None, None),
            P("chain", "sector", None, None, None),
            P("chain", None, None),
            P("chain", "sector", None, None),
            P("chain", "sector"),
        ),
        out_specs=(P("chain", "sector", None, None, None), P("chain", "sector", None, None, None)),
        check_vma=False,
    )
```

time: 517 us -> 195 us (0.38)
  the two profiles are of different devices: /device:TPU:102 before, /device:TPU:1 now
where the time goes in v2:
time: 195 us; the launch traced here: 193 us
  Pallas kernels  188 us (96%)
  other arithmetic  3.35 us (2%)
    pallas_call x1, Pallas kernels, run_layer(): pl.pallas_call(functools.partial(layer_kernel, levels, chains, sectors),...  188 us

profile of v2, /device:TPU:1, one launch (start us, length us, event | category | flops | bytes accessed | tf_op | source)
XLA Modules:
  0.0 193.1 jit_solution(10549273362257998918)
XLA Ops:
  0.6 0.0 copy-start.2
  1.3 0.0 copy-done.2
  1.3 0.6 bitcast_convert_fusion.gate_ref
  1.9 0.0 copy-start
  1.9 0.0 copy-start.1
  2.0 188.4 %shard_map.68 = (bf16[6,256,256]{2,1,0:T(8,128)(2,1)}, bf16[6,256,256]{2,1,0:T(8,128)(2,1)}) custom-call(f32[36,36]{1,0:T(8,128)} %bitcast_convert_fusion.gate_ref, s32[1,1]{1,0:T(1,128)S(6)} %copy.7.kept_ref, bf16[6,256,256]{2,1,0:T(8,128)(2,1)} %bitcast.20, bf16[1536,256]{1,0:T(8,128)(2,1)} %bitcast.22, bf16[6,256,256]{2,1,0:T(8,128)(2,1)} %bitcast.21), custom_call_target="tpu_custom_call" | custom-call | tf_op jit(solution)/shard_map/pallas_call | solution.py:261
  190.3 0.0 copy-done
  190.4 0.0 copy-done.1
  190.4 2.7 %select_bitcast_fusion = (bf16[1,1,256,6,256]{4,2,3,1,0:T(8,128)(2,1)}, bf16[1,1,256,6,256]{4,2,3,1,0:T(8,128)(2,1)}) fusion(bf16[6,256,256]{2,1,0:T(8,128)(2,1)} %get-tuple-element.5, pred[]{:T(512)S(6)} %eq.7, bf16[1,1,256,6,256]{4,2,3,1,0:T(8,128)(2,1)S(1)} %copy-done.1, bf16[6,256,256]{2,1,0:T(8,128)(2,1)} %get-tuple-element.4, ...), kind=kLoop, calls=%fused_computation | loop fusion | flops 1179648 | bytes 4718600 | tf_op jit(solution)/shard_map/broadcast_in_dim | solution.py:307
  (1 shorter events, 0.0 us)
Async XLA Ops:
  0.6 0.7 copy-start.2
  1.9 188.4 %copy-start = (bf16[1,1,256,6,256]{4,2,3,1,0:T(8,128)(2,1)S(1)}, bf16[1,1,256,6,256]{4,2,3,1,0:T(8,128)(2,1)}, u32[]{:S(2)}) copy-start(bf16[1,1,256,6,256]{4,2,3,1,0:T(8,128)(2,1)} %param.5) | copy-start | bytes 2359300
  1.9 188.4 %copy-start.1 = (bf16[1,1,256,6,256]{4,2,3,1,0:T(8,128)(2,1)S(1)}, bf16[1,1,256,6,256]{4,2,3,1,0:T(8,128)(2,1)}, u32[]{:S(2)}) copy-start(bf16[1,1,256,6,256]{4,2,3,1,0:T(8,128)(2,1)} %param.6) | copy-start | bytes 2359300

commit v3 on v2

--- a/solution.py
+++ b/solution.py
@@ -59,9 +59,9 @@
     return jnp.concatenate(tiles, axis=0)
 
 
-def invert_factor(width, work):
+def invert_factor(width, work, begin, end):
     size = work.shape[0]
-    for start in range(0, size, width):
+    for start in range(begin, end, width):
         stop = start + width
         eye = identity(width)
         reduced = eliminate(jnp.concatenate([work[start:stop, start:stop], eye], axis=1), width)
@@ -121,8 +121,15 @@
     def down_copy(hop, r):
         return remote(slot(hop - 1, r), slot(hop, r), down_send.at[hop - 1, r], down_recv.at[hop - 1, r], below[1])
 
-    def piece_copy(p):
-        return remote(pieces.at[p], left_out.at[p], piece_send.at[p - 1], piece_recv.at[p - 1], below[p])
+    def columns(part):
+        return pl.ds(part * (size // 2), size // 2)
+
+    def piece_copy(part, p):
+        target = left_out.at[p, :, columns(part)]
+        return remote(pieces.at[part, p], target, piece_send.at[part, p - 1], piece_recv.at[part, p - 1], below[p])
+
+    def own_copy(part):
+        return pltpu.make_async_copy(pieces.at[part, 0], left_out.at[0, :, columns(part)], own_sem.at[part])
 
     def fresh_copy(q):
         return remote(fresh.at[q], right_out.at[q], fresh_send.at[q], fresh_recv.at[q], after)
@@ -138,10 +145,11 @@
             if 0 <= r <= last:
                 product = jnp.dot(source[...], right_in[q, last - r], preferred_element_type=jnp.float32)
                 term = product.astype(jnp.bfloat16).astype(jnp.float32) * gate(p, q, n)
-                if n == max(0, p + q - last):
+                if (p, q) in begun:
+                    total[p, q] += term
+                else:
                     total[p, q] = term
-                else:
-                    total[p, q] += term
+                    begun.add((p, q))
 
     def finish_row(p):
         for q in range(levels):
@@ -155,63 +163,79 @@
         pl.semaphore_signal(barrier, inc=1, device_id=partner, device_id_type=MESH)
     pl.semaphore_wait(barrier, len(partners))
 
-    queue = []
-
-    def ready(hop):
-        for p in range(min(hop, near) + 1):
+    queue, here, queued, begun = [], set(), set(), set()
+    terms_left = [levels] * levels
+
+    def needs(p, n):
+        offset = n - p
+        slices = range(max(0, -offset), min(last, last - offset) + 1)
+        return {("left", p, n)} | {("right", offset, r) for r in slices}
+
+    def arrived(*what):
+        here.add(what)
+        for p in range(levels):
             for n in range(levels):
-                if max(p, abs(n - p)) == hop:
-                    queue.append(functools.partial(add_term, p, n))
-                    if n == last:
-                        queue.append(functools.partial(finish_row, p))
+                if (p, n) not in queued and needs(p, n) <= here:
+                    queued.add((p, n))
+                    queue.append((p, n))
 
     def work_on(count):
         for _ in range(min(count, len(queue))):
-            queue.pop(0)()
-
-    for r in range(levels):
+            p, n = queue.pop(0)
+            add_term(p, n)
+            terms_left[p] -= 1
+            if terms_left[p] == 0:
+                finish_row(p)
+
+    order = sorted(range(levels), key=lambda r: -max(r, last - r))
+    for r in order:
         chain_copy(r).start()
     for n in range(levels):
         left_copy(1, n).start()
-    for n in range(levels):
+        arrived("left", 0, n)
+    for n in range(2):
         far_copy(n).start()
     back_total[...] = jnp.zeros_like(back_total)
-    for r in range(levels):
+    for r in order:
         chain_copy(r).wait_recv()
         if r < last:
             down_copy(1, r).start()
         if r > 0:
             up_copy(1, r).start()
-    ready(0)
+        arrived("right", 0, r)
     for hop in range(1, levels):
+        for step in range(levels - hop):
+            up, down = last - step, step
+            up_copy(hop, up).wait_recv()
+            if up > hop:
+                up_copy(hop + 1, up).start()
+            down_copy(hop, down).wait_recv()
+            if down + hop < last:
+                down_copy(hop + 1, down).start()
+            arrived("right", -hop, up)
+            arrived("right", hop, down)
+            work_on(1)
         for n in range(levels):
             if hop <= near:
                 left_copy(hop, n).wait_recv()
                 if hop < near or n >= turned:
                     left_copy(hop + 1, n).start()
-            if n >= hop:
-                up_copy(hop, n).wait_recv()
-                if n > hop:
-                    up_copy(hop + 1, n).start()
-            if n + hop <= last:
-                down_copy(hop, n).wait_recv()
-                if n + hop < last:
-                    down_copy(hop + 1, n).start()
-            work_on(2)
-        if hop == 2:
-            for n in range(turned):
-                far_copy(n).wait_recv()
-                left_copy(near + 1, n).start()
-        ready(hop)
-    work_on(len(queue))
-    for p in range(near + 1, levels):
-        for n in range(levels):
-            if p < last:
-                left_copy(p, n).wait_recv()
+                arrived("left", hop, n)
+                if n == 0 and 2 * hop < levels:
+                    for far in range(2 * hop, min(2 * hop + 2, levels)):
+                        far_copy(far).start()
+                if hop == near and n < turned:
+                    far_copy(n).wait_recv()
+                    left_copy(near + 1, n).start()
+                    arrived("left", last, n)
+            elif hop == near + 1:
+                left_copy(hop, n).wait_recv()
+                arrived("left", hop, n)
             elif n >= turned:
                 far_copy(n).wait_recv()
-            add_term(p, n)
-        finish_row(p)
+                arrived("left", hop, n)
+            work_on(2)
+    work_on(len(queue))
 
     back = back_total[...].astype(jnp.bfloat16)
     sketch[...] = lax.dot_general(block[...], back, COLUMNS, preferred_element_type=jnp.float32)
@@ -220,20 +244,27 @@
     ridge = RIDGE_SHARE * jnp.sum(gram * eye) / size + TINY_SHIFT
     work[:, :size] = gram + ridge * eye
     work[:, size:] = eye
-    invert_factor(min(64, size), work)
-    basis = lax.dot_general(sketch[...], work[:, size:], COLUMNS, precision=HIGHEST, preferred_element_type=jnp.float32)
     scale = math.sqrt(levels * size)
-    scaled = jnp.where(iota(basis.shape, 1) < kept_ref[0, 0], basis, 0.0) * scale
-    scaled = scaled.astype(jnp.bfloat16)
-    for p in range(levels):
-        pieces[p] = scaled[p * size:(p + 1) * size]
-    for p in range(last, 0, -1):
-        piece_copy(p).start()
-    own_copy = pltpu.make_async_copy(pieces.at[0], left_out.at[0], own_sem)
-    own_copy.start()
-    new_right = lax.dot_general(scaled, block[...], ROWS, preferred_element_type=jnp.float32) * (1.0 / scale)
+    half = size // 2
+    for part in range(2):
+        begin = part * half
+        invert_factor(min(64, half), work, begin, begin + half)
+        basis = lax.dot_general(
+            sketch[:, :begin + half], work[begin:begin + half, size:size + begin + half], COLUMNS,
+            precision=HIGHEST, preferred_element_type=jnp.float32,
+        )
+        scaled = jnp.where(iota(basis.shape, 1) + begin < kept_ref[0, 0], basis, 0.0) * scale
+        for p in range(levels):
+            pieces[part, p] = scaled[p * size:(p + 1) * size].astype(jnp.bfloat16)
+        for p in range(last, 0, -1):
+            piece_copy(part, p).start()
+        own_copy(part).start()
+    for part in range(2):
+        scaled = pieces[part].reshape(levels * size, half)
+        new_right = lax.dot_general(scaled, block[...], ROWS, preferred_element_type=jnp.float32) * (1.0 / scale)
+        for q in range(levels):
+            fresh[q, part * half:(part + 1) * half] = new_right[:, q * size:(q + 1) * size].astype(jnp.bfloat16)
     for q in range(levels):
-        fresh[q] = new_right[:, q * size:(q + 1) * size].astype(jnp.bfloat16)
         fresh_copy(q).start()
     for r in range(levels):
         chain_copy(r).wait_send()
@@ -246,17 +277,19 @@
                 down_copy(hop, r).wait_send()
             if r >= hop:
                 up_copy(hop, r).wait_send()
-    own_copy.wait()
     for q in range(levels):
         fresh_copy(q).wait()
-    for p in range(1, levels):
-        piece_copy(p).wait()
+    for part in range(2):
+        own_copy(part).wait()
+        for p in range(1, levels):
+            piece_copy(part, p).wait()
 
 
 def run_layer(gates, kept, left, right, test_matrix, chains, sectors):
     levels, size = left.shape[0], left.shape[1]
     hops = pltpu.SemaphoreType.DMA((levels - 1, levels))
     one = pltpu.SemaphoreType.DMA((levels,))
+    halves = pltpu.SemaphoreType.DMA((2, levels - 1))
     part = (levels, size, size)
     return pl.pallas_call(
         functools.partial(layer_kernel, levels, chains, sectors),
@@ -277,10 +310,10 @@
             pltpu.VMEM((size, levels * size), jnp.float32),
             pltpu.VMEM((levels * size, size), jnp.float32),
             pltpu.VMEM((size, 2 * size), jnp.float32),
+            pltpu.VMEM((2, levels, size, size // 2), jnp.bfloat16),
             pltpu.VMEM(part, jnp.bfloat16),
-            pltpu.VMEM(part, jnp.bfloat16),
-            one, one, hops, hops, one, one, hops, hops, hops, hops, one, one, one, one,
-            pltpu.SemaphoreType.DMA,
+            one, one, hops, hops, one, one, hops, hops, hops, hops, halves, halves, one, one,
+            pltpu.SemaphoreType.DMA((2,)),
         ],
         compiler_params=pltpu.CompilerParams(
             collective_id=0, has_side_effects=True, vmem_limit_bytes=VMEM_LIMIT

time: 195 us -> 176 us (0.903)
  Pallas kernels: 188 us -> 171 us
    pallas_call x1, Pallas kernels: 188 us -> 171 us  [run_layer(): pl.pallas_call(functools.partial(layer_kernel, levels, chains, sectors),...]
where the time goes in v3:
time: 176 us; the launch traced here: 175 us
  Pallas kernels  171 us (97%)
  other arithmetic  3.35 us (2%)
    pallas_call x1, Pallas kernels, run_layer(): pl.pallas_call(functools.partial(layer_kernel, levels, chains, sectors),...  171 us

profile of v3, /device:TPU:1, one launch (start us, length us, event | category | flops | bytes accessed | tf_op | source)
XLA Modules:
  0.0 175.3 jit_solution(2036114539887125053)
XLA Ops:
  0.6 0.0 copy-start.2
  1.3 0.0 copy-done.2
  1.3 0.6 bitcast_convert_fusion.gate_ref
  1.9 0.0 copy-start
  1.9 0.0 copy-start.1
  2.0 170.6 %shard_map.68 = (bf16[6,256,256]{2,1,0:T(8,128)(2,1)}, bf16[6,256,256]{2,1,0:T(8,128)(2,1)}) custom-call(f32[36,36]{1,0:T(8,128)} %bitcast_convert_fusion.gate_ref, s32[1,1]{1,0:T(1,128)S(6)} %copy.7.kept_ref, bf16[6,256,256]{2,1,0:T(8,128)(2,1)} %bitcast.20, bf16[1536,256]{1,0:T(8,128)(2,1)} %bitcast.22, bf16[6,256,256]{2,1,0:T(8,128)(2,1)} %bitcast.21), custom_call_target="tpu_custom_call" | custom-call | tf_op jit(solution)/shard_map/pallas_call | solution.py:294
  172.6 0.0 copy-done
  172.6 0.0 copy-done.1
  172.6 2.7 %select_bitcast_fusion = (bf16[1,1,256,6,256]{4,2,3,1,0:T(8,128)(2,1)}, bf16[1,1,256,6,256]{4,2,3,1,0:T(8,128)(2,1)}) fusion(bf16[6,256,256]{2,1,0:T(8,128)(2,1)} %get-tuple-element.5, pred[]{:T(512)S(6)} %eq.7, bf16[1,1,256,6,256]{4,2,3,1,0:T(8,128)(2,1)S(1)} %copy-done.1, bf16[6,256,256]{2,1,0:T(8,128)(2,1)} %get-tuple-element.4, ...), kind=kLoop, calls=%fused_computation | loop fusion | flops 1179648 | bytes 4718600 | tf_op jit(solution)/shard_map/broadcast_in_dim | solution.py:340
  (1 shorter events, 0.0 us)
Async XLA Ops:
  0.6 0.7 copy-start.2
  1.9 170.6 %copy-start = (bf16[1,1,256,6,256]{4,2,3,1,0:T(8,128)(2,1)S(1)}, bf16[1,1,256,6,256]{4,2,3,1,0:T(8,128)(2,1)}, u32[]{:S(2)}) copy-start(bf16[1,1,256,6,256]{4,2,3,1,0:T(8,128)(2,1)} %param.5) | copy-start | bytes 2359300
  1.9 170.6 %copy-start.1 = (bf16[1,1,256,6,256]{4,2,3,1,0:T(8,128)(2,1)S(1)}, bf16[1,1,256,6,256]{4,2,3,1,0:T(8,128)(2,1)}, u32[]{:S(2)}) copy-start(bf16[1,1,256,6,256]{4,2,3,1,0:T(8,128)(2,1)} %param.6) | copy-start | bytes 2359300

commit v4 on v3

v4 whole, which is shorter than its diff:
```python
import functools
import math

import jax
import jax.numpy as jnp
from jax import lax
from jax.experimental import pallas as pl
from jax.experimental.pallas import tpu as pltpu
from jax.sharding import PartitionSpec as P

RIDGE_SHARE = 0.05
TINY_SHIFT = 1e-05
MESH = pl.DeviceIdType.MESH
HIGHEST = lax.Precision.HIGHEST
VMEM_LIMIT = 56 * 1024 * 1024
ROWS = (((0,), (0,)), ((), ()))
COLUMNS = (((1,), (1,)), ((), ()))


def ring(index, by, size):
    return lax.rem(index + (by + size), size)


def iota(shape, dim):
    return lax.broadcasted_iota(jnp.int32, shape, dim)


def identity(size):
    return jnp.where(iota((size, size), 0) == iota((size, size), 1), 1.0, 0.0)


def eliminate(local, width):
    shape = (8, 2 * width)
    tiles = [local[8 * t:8 * (t + 1)] for t in range(width // 8)]
    index = iota(shape, 0)
    for t0 in range(width // 8):
        columns = [
            [jnp.broadcast_to(tile[:, 8 * t0 + j:8 * t0 + j + 1], shape) for tile in tiles[t0:]] for j in range(8)
        ]
        rows = [jnp.broadcast_to(tiles[t0][j:j + 1], shape) for j in range(8)]
        pivots = [[jnp.broadcast_to(columns[l][0][j:j + 1], shape) for l in range(j + 1)] for j in range(8)]
        scaled = []
        for j in range(8):
            inverse = 1.0 / pivots[j][j]
            for i in range(j + 1, 8):
                share = pivots[i][j] * inverse
                for l in range(j + 1, i + 1):
                    pivots[i][l] = pivots[i][l] - share * pivots[l][j]
                rows[i] = rows[i] - share * rows[j]
                columns[i] = [x - share * y for x, y in zip(columns[i], columns[j])]
            scaled.append(rows[j] * inverse)
        kept = tiles[t0]
        for j in range(1, 8):
            kept = jnp.where(index == j, rows[j], kept)
        tiles[t0] = kept
        for t in range(t0 + 1, width // 8):
            for j in range(8):
                tiles[t] = tiles[t] - columns[j][t - t0] * scaled[j]
    return jnp.concatenate(tiles, axis=0)


def invert_factor(width, work, begin, end):
    size = work.shape[0]
    for start in range(begin, end, width):
        stop = start + width
        eye = identity(width)
        reduced = eliminate(jnp.concatenate([work[start:stop, start:stop], eye], axis=1), width)
        pivots = jnp.sum(reduced[:, :width] * eye, axis=1, keepdims=True)
        small = reduced[:, width:] * lax.rsqrt(pivots)
        top = jnp.dot(small, work[start:stop, begin:], precision=HIGHEST, preferred_element_type=jnp.float32)
        work[start:stop, begin:] = top
        if stop < end:
            work[stop:end, begin:] -= lax.dot_general(
                top[:, stop - begin:end - begin], top, ROWS, precision=HIGHEST, preferred_element_type=jnp.float32
            )


def layer_kernel(
    levels, chains, sectors,
    gate_ref, kept_ref, left_ref, test_ref, right_ref,
    left_out, right_out,
    test_in, kept_in, left_in, right_in, lowest, total, block, back_total, sketch, work, pieces, fresh,
    chain_send, chain_recv, test_send, test_recv, kept_send, kept_recv, left_send, left_recv, up_send, up_recv, down_send, down_recv,
    piece_send, piece_recv, fresh_send, fresh_recv, own_sem,
):
    chain, sector = lax.axis_index("chain"), lax.axis_index("sector")
    above = [(chain, ring(sector, p, sectors)) for p in range(levels)]
    below = [(chain, ring(sector, -p, sectors)) for p in range(levels)]
    before = (ring(chain, -1, chains), sector)
    after = (ring(chain, 1, chains), sector)
    owner = (ring(chain, 1, chains), ring(sector, 1, sectors))
    maker = (ring(chain, -1, chains), ring(sector, -1, sectors))
    partners = (before, after, owner, maker, *above[1:levels - 1], *below[1:levels - 1])
    middle = ring(sector, 1, sectors)
    last = levels - 1
    size = left_ref.shape[1]

    def remote(source, target, send_sem, recv_sem, device):
        return pltpu.make_async_remote_copy(
            src_ref=source, dst_ref=target, send_sem=send_sem, recv_sem=recv_sem, device_id=device, device_id_type=MESH
        )

    def slot(offset, r):
        return right_in.at[r + offset, last - r]

    def place(offset, r):
        return lowest if offset + r < 0 else slot(offset, r)

    def chain_copy(r):
        return remote(right_ref.at[r], place(-1, r), chain_send.at[r], chain_recv.at[r], before)

    def left_at(p, n):
        return left_ref.at[n] if p == 1 else left_in.at[p, n]

    def left_copy(p, n):
        source, device = (left_at(1, n), below[1]) if p == 0 else (left_at(p - 1, n), above[1])
        return remote(source, left_in.at[p, n], left_send.at[p, n], left_recv.at[p, n], device)

    def up_copy(offset, r):
        sems = up_send.at[-offset, r], up_recv.at[-offset, r]
        return remote(slot(offset + 1, r), slot(offset, r), *sems, above[1])

    def down_copy(offset, r):
        sems = down_send.at[offset, r], down_recv.at[offset, r]
        return remote(place(offset - 1, r), slot(offset, r), *sems, below[1])

    def test_copy(n):
        rows = pl.ds(n * size, size)
        return remote(test_ref.at[rows], test_in.at[rows], test_send.at[n], test_recv.at[n], below[1])

    kept_copy = remote(kept_ref, kept_in, kept_send, kept_recv, below[1])

    def columns(part):
        return pl.ds(part * (size // 2), size // 2)

    def piece_copy(part, p):
        target, sems = left_out.at[p, :, columns(part)], (piece_send.at[part, p], piece_recv.at[part, p])
        return remote(pieces.at[part, p], target, *sems, above[1] if p == 0 else below[p - 1])

    def own_copy(part):
        return pltpu.make_async_copy(pieces.at[part, 1], left_out.at[1, :, columns(part)], own_sem.at[part])

    def fresh_copy(part, q):
        target = right_out.at[q, columns(part)]
        return remote(fresh.at[part, q], target, fresh_send.at[part, q], fresh_recv.at[part, q], owner)

    def gate(p, q, n):
        inside = (middle >= p) & (middle + q < sectors)
        return jnp.where(inside, gate_ref[p * levels + q, n * levels + p + q - n], 0.0)

    def add_term(p, n):
        source = left_at(p, n)
        for q in range(levels):
            r = p + q - n
            if 0 <= r <= last:
                product = jnp.dot(source[...], right_in[q, last - r], preferred_element_type=jnp.float32)
                term = product.astype(jnp.bfloat16).astype(jnp.float32) * gate(p, q, n)
                if (p, q) in begun:
                    total[p, q] += term
                else:
                    total[p, q] = term
                    begun.add((p, q))

    def finish_row(p):
        for q in range(levels):
            block[p * size:(p + 1) * size, q * size:(q + 1) * size] = total[p, q].astype(jnp.bfloat16)
        row = block[p * size:(p + 1) * size, :]
        first = jnp.dot(row, test_in[...], preferred_element_type=jnp.float32).astype(jnp.bfloat16)
        back_total[...] += lax.dot_general(first, row, ROWS, preferred_element_type=jnp.float32)

    barrier = pltpu.get_barrier_semaphore()
    for partner in partners:
        pl.semaphore_signal(barrier, inc=1, device_id=partner, device_id_type=MESH)
    pl.semaphore_wait(barrier, len(partners))

    queue, here, queued, begun = [], set(), set(), set()
    terms_left = [levels] * levels

    def needs(p, n):
        offset = n - p
        slices = range(max(0, -offset), min(last, last - offset) + 1)
        return {("left", p, n)} | {("right", offset, r) for r in slices}

    def arrived(*what):
        here.add(what)
        for p in range(levels):
            for n in range(levels):
                if (p, n) not in queued and needs(p, n) <= here:
                    queued.add((p, n))
                    queue.append((p, n))

    def work_on(count):
        for _ in range(min(count, len(queue))):
            p, n = queue.pop(0)
            add_term(p, n)
            terms_left[p] -= 1
            if terms_left[p] == 0:
                finish_row(p)

    def left_steps(p, chunks):
        for n in chunks:
            left_copy(p, n).wait_recv()
            if 1 < p < last:
                left_copy(p + 1, n).start()
            arrived("left", p, n)
            work_on(2)

    def up_step(offset, r):
        up_copy(offset, r).wait_recv()
        if r > -offset:
            up_copy(offset - 1, r).start()
        arrived("right", offset, r)

    def down_step(offset, r):
        down_copy(offset, r).wait_recv()
        if r + offset < last:
            down_copy(offset + 1, r).start()
        arrived("right", offset, r)

    def right_steps(hop):
        for step in range(levels + 1 - hop):
            down_step(hop - 1, step)
            if hop < last and last - step > hop:
                up_step(-1 - hop, last - step)
            work_on(1)

    order = sorted(range(levels), key=lambda r: -max(r - 1, levels - r))
    for r in order:
        chain_copy(r).start()
    for n in range(levels):
        left_copy(2, n).start()
        left_copy(0, n).start()
        arrived("left", 1, n)
    kept_copy.start()
    back_total[...] = jnp.zeros_like(back_total)
    for r in order:
        chain_copy(r).wait_recv()
        down_copy(0, r).start()
        if r > 1:
            up_copy(-2, r).start()
        arrived("right", -1, r)
    for n in range(levels):
        left_steps(2, [n])
        left_steps(0, [n])
    right_steps(1)
    for n in range(levels):
        test_copy(n).start()
    for hop in range(2, last - 1):
        right_steps(hop)
        if hop == 3:
            for n in range(levels):
                test_copy(n).wait_recv()
        left_steps(hop + 1, range(levels))
    right_steps(last - 1)
    left_steps(last, range(levels // 3))
    right_steps(last)
    left_steps(last, range(levels // 3, 2 * levels // 3))
    right_steps(levels)
    left_steps(last, range(2 * levels // 3, levels))
    work_on(len(queue))
    kept_copy.wait_recv()

    back = back_total[...].astype(jnp.bfloat16)
    sketch[...] = lax.dot_general(block[...], back, COLUMNS, preferred_element_type=jnp.float32)
    scale = math.sqrt(levels * size)
    half = size // 2
    ridge = RIDGE_SHARE * jnp.sum(sketch[...] * sketch[...]) / size + TINY_SHIFT

    def load_gram(begin):
        gram = lax.dot_general(
            sketch[:, begin:begin + half], sketch[:, begin:], ROWS, precision=HIGHEST, preferred_element_type=jnp.float32
        )
        shape = (half, size - begin)
        work[begin:begin + half, begin:size] = gram + jnp.where(iota(shape, 0) == iota(shape, 1), ridge, 0.0)
        shape = (half, size)
        work[begin:begin + half, size:] = jnp.where(iota(shape, 0) + begin == iota(shape, 1), 1.0, 0.0)

    def send_pieces(part):
        begin = part * half
        basis = lax.dot_general(
            sketch[:, :begin + half], work[begin:begin + half, size:size + begin + half], COLUMNS,
            precision=HIGHEST, preferred_element_type=jnp.float32,
        )
        scaled = jnp.where(iota(basis.shape, 1) + begin < kept_in[0:1, :half], basis, 0.0) * scale
        for p in range(levels):
            pieces[part, p] = scaled[p * size:(p + 1) * size].astype(jnp.bfloat16)
        for p in (*range(last, 2, -1), 0, 2):
            piece_copy(part, p).start()
        own_copy(part).start()

    def send_fresh(part):
        scaled = pieces[part].reshape(levels * size, half)
        new_right = lax.dot_general(scaled, block[...], ROWS, preferred_element_type=jnp.float32) * (1.0 / scale)
        for q in range(levels):
            fresh[part, q] = new_right[:, q * size:(q + 1) * size].astype(jnp.bfloat16)
            fresh_copy(part, q).start()

    load_gram(0)
    invert_factor(min(64, half), work, 0, half)
    send_pieces(0)
    send_fresh(0)
    load_gram(half)
    top = work[:half, half:]
    work[half:, half:] -= lax.dot_general(
        top[:, :half], top, ROWS, precision=HIGHEST, preferred_element_type=jnp.float32
    )
    invert_factor(min(64, half), work, half, size)
    send_pieces(1)
    send_fresh(1)
    kept_copy.wait_send()
    for r in range(levels):
        chain_copy(r).wait_send()
        test_copy(r).wait_send()
        for p in range(levels):
            if p != 1:
                left_copy(p, r).wait_send()
        for offset in range(levels - r):
            down_copy(offset, r).wait_send()
        for offset in range(-r, -1):
            up_copy(offset, r).wait_send()
    for part in range(2):
        own_copy(part).wait()
        for q in range(levels):
            fresh_copy(part, q).wait()
        for p in range(levels):
            if p != 1:
                piece_copy(part, p).wait()


def run_layer(gates, kept, left, right, test_matrix, chains, sectors):
    levels, size = left.shape[0], left.shape[1]
    square = pltpu.SemaphoreType.DMA((levels, levels))
    scalar = pltpu.SemaphoreType.DMA
    one = pltpu.SemaphoreType.DMA((levels,))
    two = pltpu.SemaphoreType.DMA((2,))
    both = pltpu.SemaphoreType.DMA((2, levels))
    part = (levels, size, size)
    return pl.pallas_call(
        functools.partial(layer_kernel, levels, chains, sectors),
        out_shape=(jax.ShapeDtypeStruct(part, jnp.bfloat16), jax.ShapeDtypeStruct(part, jnp.bfloat16)),
        in_specs=[
            pl.BlockSpec(memory_space=pltpu.SMEM),
            pl.BlockSpec(memory_space=pltpu.VMEM),
            pl.BlockSpec(memory_space=pltpu.VMEM),
            pl.BlockSpec(memory_space=pl.ANY),
            pl.BlockSpec(memory_space=pl.ANY),
        ],
        out_specs=(pl.BlockSpec(memory_space=pl.ANY),) * 2,
        scratch_shapes=[
            pltpu.VMEM((levels * size, size), jnp.bfloat16),
            pltpu.VMEM(kept.shape, jnp.int32),
            pltpu.VMEM((levels, *part), jnp.bfloat16),
            pltpu.VMEM((levels, *part), jnp.bfloat16),
            pltpu.VMEM((size, size), jnp.bfloat16),
            pltpu.VMEM((levels, *part), jnp.float32),
            pltpu.VMEM((levels * size, levels * size), jnp.bfloat16),
            pltpu.VMEM((size, levels * size), jnp.float32),
            pltpu.VMEM((levels * size, size), jnp.float32),
            pltpu.VMEM((size, 2 * size), jnp.float32),
            pltpu.VMEM((2, levels, size, size // 2), jnp.bfloat16),
            pltpu.VMEM((2, levels, size // 2, size), jnp.bfloat16),
            one, one, one, one, scalar, scalar, square, square, square, square, square, square, both, both, both, both, two,
        ],
        compiler_params=pltpu.CompilerParams(
            collective_id=0, has_side_effects=True, vmem_limit_bytes=VMEM_LIMIT
        ),
    )(gates, kept, left, test_matrix, right)


def per_device(left_sites, right_sites, pair_gates, test_matrix, kept_columns):
    sectors = lax.axis_size("sector")
    sector = lax.axis_index("sector")
    chains = lax.axis_size("chain")
    chain = lax.axis_index("chain")
    left = jnp.transpose(left_sites[0, 0], (1, 0, 2))
    right = jnp.transpose(right_sites[0, 0], (1, 0, 2))
    gates = pair_gates[0].astype(jnp.float32)
    kept = jnp.broadcast_to(kept_columns, (8, 128))
    fresh_left, shipped = run_layer(gates, kept, left, right, test_matrix[0, 0], chains, sectors)
    inside = sector + jnp.arange(left.shape[0])[:, None, None] < sectors
    fresh_left = jnp.where(inside, fresh_left, jnp.zeros_like(fresh_left))
    new_left = jnp.where(chain == chains - 1, left, fresh_left)
    new_right = jnp.where(chain == 0, right, shipped)
    return (
        jnp.transpose(new_left, (1, 0, 2))[None, None],
        jnp.transpose(new_right, (1, 0, 2))[None, None],
    )


def solution(mesh):
    return jax.shard_map(
        per_device,
        mesh=mesh,
        in_specs=(
            P("chain", "sector", None, None, None),
            P("chain", "sector", None, None, None),
            P("chain", None, None),
            P("chain", "sector", None, None),
            P("chain", "sector"),
        ),
        out_specs=(P("chain", "sector", None, None, None), P("chain", "sector", None, None, None)),
        check_vma=False,
    )
```

time: 176 us -> 160 us (0.909)
  Pallas kernels: 171 us -> 154 us
    pallas_call x1, Pallas kernels: 171 us -> 154 us  [run_layer(): pl.pallas_call(functools.partial(layer_kernel, levels, chains, sectors),...]
where the time goes in v4:
time: 160 us
  Pallas kernels  154 us (96%)
  other arithmetic  3.35 us (2%)
    pallas_call x1, Pallas kernels, run_layer(): pl.pallas_call(functools.partial(layer_kernel, levels, chains, sectors),...  154 us

profile of v4, /device:TPU:1, one launch (start us, length us, event | category | flops | bytes accessed | tf_op | source)
XLA Modules:
  0.0 159.7 jit_solution(10179134139007656603)
XLA Ops:
  0.6 0.0 copy-start.2
  1.3 0.6 broadcast_in_dim.27.kept_ref
  1.9 0.0 copy-done.2
  1.9 0.6 bitcast_convert_fusion.gate_ref
  2.5 0.0 copy-start
  2.5 0.0 copy-start.1
  2.5 154.4 %shard_map.68 = (bf16[6,256,256]{2,1,0:T(8,128)(2,1)}, bf16[6,256,256]{2,1,0:T(8,128)(2,1)}) custom-call(f32[36,36]{1,0:T(8,128)} %bitcast_convert_fusion.gate_ref, s32[8,128]{1,0:T(8,128)} %broadcast_in_dim.27.kept_ref, bf16[6,256,256]{2,1,0:T(8,128)(2,1)} %bitcast.22, bf16[1536,256]{1,0:T(8,128)(2,1)} %bitcast.24, bf16[6,256,256]{2,1,0:T(8,128)(2,1)} %bitcast.23), custom_call_target="tpu_custom_call" | custom-call | tf_op jit(solution)/shard_map/pallas_call | solution.py:338
  157.0 0.0 copy-done
  157.0 0.0 copy-done.1
  157.0 2.7 %select_bitcast_fusion = (bf16[1,1,256,6,256]{4,2,3,1,0:T(8,128)(2,1)}, bf16[1,1,256,6,256]{4,2,3,1,0:T(8,128)(2,1)}) fusion(bf16[6,256,256]{2,1,0:T(8,128)(2,1)} %get-tuple-element.5, pred[]{:T(512)S(6)} %eq.7, bf16[1,1,256,6,256]{4,2,3,1,0:T(8,128)(2,1)S(1)} %copy-done.1, bf16[6,256,256]{2,1,0:T(8,128)(2,1)} %get-tuple-element.4, ...), kind=kLoop, calls=%fused_computation | loop fusion | flops 1179648 | bytes 4718600 | tf_op jit(solution)/shard_map/broadcast_in_dim | solution.py:386
  (1 shorter events, 0.0 us)
Async XLA Ops:
  0.6 1.3 copy-start.2
  2.5 154.5 %copy-start = (bf16[1,1,256,6,256]{4,2,3,1,0:T(8,128)(2,1)S(1)}, bf16[1,1,256,6,256]{4,2,3,1,0:T(8,128)(2,1)}, u32[]{:S(2)}) copy-start(bf16[1,1,256,6,256]{4,2,3,1,0:T(8,128)(2,1)} %param.5) | copy-start | bytes 2359300
  2.5 154.5 %copy-start.1 = (bf16[1,1,256,6,256]{4,2,3,1,0:T(8,128)(2,1)S(1)}, bf16[1,1,256,6,256]{4,2,3,1,0:T(8,128)(2,1)}, u32[]{:S(2)}) copy-start(bf16[1,1,256,6,256]{4,2,3,1,0:T(8,128)(2,1)} %param.6) | copy-start | bytes 2359300
